TPU v7x, 32 devices: a whole 2x2x4 slice. The times are simulated.
32 devices in a mesh: tower: 2 (over x), dp: 16 (over z, y, core).
Axes of the slice: x: 2, y: 2, z: 4, core: 2. Of those that a mesh axis runs over, the one named last changes fastest.
Arguments:
- tokens: bfloat16 [24576, 768], P(('tower', 'dp')), may hold values from -6 to 6
- cotangent: bfloat16 [24576, 768], P(('tower', 'dp')), may hold values from -6 to 6
- caption_lengths: int32 [32, 24], P(('tower', 'dp')), may hold values from 1 to 64, 768 in all within a row
- image_index: int32 [32, 24], P(('tower', 'dp')), may hold values from 0 to 3
- image_states: bfloat16 [128, 576, 768], P(('tower', 'dp')), may hold values from -6 to 6
- master_weights: float32 [12288, 768], P(('tower', 'dp')), as said below
- first_moments: float32 [12288, 768], P(('tower', 'dp')), as said below
- second_moments: float32 [12288, 768], P(('tower', 'dp')), as said below
- owner_list: int32 [64], replicated, may hold values from 0 to 63, as said below
- norm_params: float32 [8, 768], replicated, as said below
- norm_first: float32 [8, 768], replicated, as said below
- norm_second: float32 [8, 768], replicated, as said below
Outputs:
- layer_out: bfloat16 [24576, 768], P(('tower', 'dp'))
- grad_tokens: float32 [24576, 768], P(('tower', 'dp'))
- grad_images: float32 [128, 576, 768], P(('tower', 'dp'))
- new_weights: float32 [12288, 768], P(('tower', 'dp'))
- new_first: float32 [12288, 768], P(('tower', 'dp'))
- new_second: float32 [12288, 768], P(('tower', 'dp'))
- weight_copy: bfloat16 [12288, 768], P(('tower', 'dp'))
- norm_new: float32 [8, 768], replicated
- norm_first_new: float32 [8, 768], replicated
- norm_second_new: float32 [8, 768], replicated
Inputs may be any that keep to these rules, and one draw needn't show every extreme that they name: `caption_lengths`: each row holds one device's 24 caption lengths, summing to 768, the longest exactly 64. `owner_list`: a permutation of the 64 groups. `master_weights`: weights of the scale of their fan-in. `first_moments`: both signs. `second_moments`: positive. `norm_params`: gains near one, biases of both signs. `norm_first`: both signs. `norm_second`: positive.
All inputs are finite; a program needn't handle non-finite values.
Results may differ from a plain program's by a relative error of at most 0.02.
Values may be sent and summed in bfloat16 or wider, within the bound.
A program may use at most 384 MiB of HBM per device.

v0:
```python
import jax
import jax.numpy as jnp
from jax import lax
from jax.sharding import PartitionSpec as P

D = 768
HEADS = 12
HDIM = 64
FF = 3072
MAXLEN = 64
STEP = 5


beta_one = 0.5
beta_two = 0.6
learn_rate = 0.03
norm_rate = 0.4
weight_decay = 0.01
epsilon = 1e-08
norm_eps = 1e-05
masked_score = -1000000000.0


def from_partner(block, axis, distance):
    count = lax.axis_size(axis)
    route = []
    for low in range(count):
        high = low | 1 << distance
        if high != low and high < count:
            route += [(low, high), (high, low)]
    return lax.ppermute(block, axis, route)


def norm_forward(inputs, gains, shifts):
    average = jnp.mean(inputs, axis=-1, keepdims=True)
    centred = inputs - average
    inv_std = lax.rsqrt(jnp.mean(centred * centred, axis=-1, keepdims=True) + norm_eps)
    normed = centred * inv_std
    return (normed * gains + shifts, normed, inv_std)


def norm_backward(grad_out, normed, inv_std, gains):
    sum_axes = tuple(range(grad_out.ndim - 1))
    grad_normed = grad_out * gains
    grad_gain = jnp.sum(grad_out * normed, axis=sum_axes)
    grad_shift = jnp.sum(grad_out, axis=sum_axes)
    grad_in = inv_std * (
        grad_normed
        - jnp.mean(grad_normed, axis=-1, keepdims=True)
        - normed * jnp.mean(grad_normed * normed, axis=-1, keepdims=True)
    )
    return (grad_in, grad_gain, grad_shift)


def project(left, right):
    return jnp.dot(left, right, preferred_element_type=jnp.float32)


def times_trans(left, right):
    return lax.dot_general(
        left, right, (((1,), (1,)), ((), ())), preferred_element_type=jnp.float32
    )


def weight_grad(left, right):
    return lax.dot_general(
        left, right, (((0,), (0,)), ((), ())), preferred_element_type=jnp.float32
    )


def row_softmax(scores):
    row_top = jnp.max(scores, axis=-1, keepdims=True)
    exponent = jnp.exp(scores - row_top)
    row_total = jnp.sum(exponent, axis=-1, keepdims=True)
    return (exponent / row_total, row_top + jnp.log(row_total))


def attend_back(query, keys, values, probs, grad_att, score_scale):
    probs_low = probs.astype(jnp.bfloat16)
    grad_values = jnp.einsum(
        "hqk,qhd->khd", probs_low, grad_att, preferred_element_type=jnp.float32
    )
    grad_probs = jnp.einsum("qhd,khd->hqk", grad_att, values, preferred_element_type=jnp.float32)
    grad_scores = (
        probs * (grad_probs - jnp.sum(grad_probs * probs, axis=-1, keepdims=True))
    ).astype(jnp.bfloat16)
    grad_query = (
        jnp.einsum("hqk,khd->qhd", grad_scores, keys, preferred_element_type=jnp.float32)
        * score_scale
    )
    grad_keys = (
        jnp.einsum("hqk,qhd->khd", grad_scores, query, preferred_element_type=jnp.float32)
        * score_scale
    )
    return (grad_query, grad_keys, grad_values)


def split_rows(packed):
    pieces = [packed[index_row * D : (index_row + 1) * D] for index_row in range(8)]
    return tuple(pieces) + (packed[8 * D : 8 * D + FF], packed[8 * D + FF : 8 * D + 2 * FF])


def adamw_update(weight, moment, second, grad_in, rate, decay_rate):
    new_moment = beta_one * moment + (1.0 - beta_one) * grad_in
    new_second = beta_two * second + (1.0 - beta_two) * grad_in * grad_in
    moment_hat = new_moment / (1.0 - beta_one**STEP)
    second_hat = new_second / (1.0 - beta_two**STEP)
    new_weight = weight - rate * (
        moment_hat / (jnp.sqrt(second_hat) + epsilon) + decay_rate * weight
    )
    return (new_weight, new_moment, new_second)


def per_device(
    tokens,
    cotangent,
    caption_lengths,
    image_index,
    image_states,
    master_weights,
    first_moments,
    second_moments,
    owner_list,
    norm_params,
    norm_first,
    norm_second,
):
    tok_rows = tokens.shape[0]
    groups = owner_list.shape[0]
    total_rows = 8 * D + 2 * FF
    group_rows = total_rows // groups
    images_dev = image_states.shape[0]
    patches = image_states.shape[1]
    score_scale = HDIM ** (-0.5)
    slot_weights = lax.all_gather(
        master_weights.astype(jnp.bfloat16), ("tower", "dp"), axis=0, tiled=True
    )
    inverse = jnp.argsort(owner_list)
    logical = slot_weights.reshape(groups, group_rows, D)[inverse].reshape(total_rows, D)
    w_query, w_key, w_value, w_output, c_query, c_key, c_value, c_output, up_rows, down_rows = (
        split_rows(logical)
    )
    images = image_states.astype(jnp.float32)
    encoded, enc_normed, enc_inv = norm_forward(images, norm_params[3], norm_params[7])
    arrived = from_partner(encoded.astype(jnp.bfloat16), "tower", 0)
    lengths = caption_lengths[0]
    picks = image_index[0]
    ends = jnp.cumsum(lengths)
    starts = ends - lengths
    positions = jnp.arange(tok_rows, dtype=jnp.int32)
    segment = jnp.sum((positions[:, None] >= ends[None, :]).astype(jnp.int32), axis=1)
    token_slot = positions - jnp.take(starts, segment)
    slot_ids = jnp.arange(MAXLEN, dtype=jnp.int32)
    pad_index = jnp.minimum(starts[:, None] + slot_ids[None, :], tok_rows - 1)
    slot_valid = slot_ids[None, :] < lengths[:, None]
    image_ids = jnp.arange(images_dev, dtype=jnp.int32)
    caption_onehot = (picks[:, None] == image_ids[None, :]).astype(jnp.float32)
    same_doc = (segment[:, None] == segment[None, :]) & (positions[None, :] <= positions[:, None])
    inputs = tokens.astype(jnp.float32)
    first_out, first_normed, first_inv = norm_forward(inputs, norm_params[0], norm_params[4])
    first_low = first_out.astype(jnp.bfloat16)
    query = project(first_low, w_query).astype(jnp.bfloat16).reshape(tok_rows, HEADS, HDIM)
    keys = project(first_low, w_key).astype(jnp.bfloat16).reshape(tok_rows, HEADS, HDIM)
    values = project(first_low, w_value).astype(jnp.bfloat16).reshape(tok_rows, HEADS, HDIM)
    raw = jnp.einsum("qhd,khd->hqk", query, keys, preferred_element_type=jnp.float32) * score_scale
    masked = jnp.where(same_doc[None], raw, masked_score)
    probs, self_lse = row_softmax(masked)
    attended = jnp.einsum(
        "hqk,khd->qhd", probs.astype(jnp.bfloat16), values, preferred_element_type=jnp.float32
    )
    attended_low = attended.astype(jnp.bfloat16).reshape(tok_rows, D)
    resid_one = inputs + project(attended_low, w_output)
    second_out, second_normed, second_inv = norm_forward(resid_one, norm_params[1], norm_params[5])
    second_low = second_out.astype(jnp.bfloat16)
    cross_query = project(second_low, c_query).astype(jnp.bfloat16).reshape(tok_rows, HEADS, HDIM)
    cross_keys = (
        jnp.einsum("ipd,de->ipe", arrived, c_key, preferred_element_type=jnp.float32)
        .astype(jnp.bfloat16)
        .reshape(images_dev, patches, HEADS, HDIM)
    )
    cross_values = (
        jnp.einsum("ipd,de->ipe", arrived, c_value, preferred_element_type=jnp.float32)
        .astype(jnp.bfloat16)
        .reshape(images_dev, patches, HEADS, HDIM)
    )
    caption_query = cross_query[pad_index]
    caption_keys = cross_keys[picks]
    caption_values = cross_values[picks]
    cross_raw = (
        jnp.einsum(
            "cqhd,ckhd->chqk", caption_query, caption_keys, preferred_element_type=jnp.float32
        )
        * score_scale
    )
    cross_probs, cross_lse = row_softmax(cross_raw)
    caption_out = jnp.einsum(
        "chqk,ckhd->cqhd",
        cross_probs.astype(jnp.bfloat16),
        caption_values,
        preferred_element_type=jnp.float32,
    )
    cross_sum = caption_out[segment, token_slot]
    cross_low = cross_sum.astype(jnp.bfloat16).reshape(tok_rows, D)
    resid_two = resid_one + project(cross_low, c_output)
    third_out, third_normed, third_inv = norm_forward(resid_two, norm_params[2], norm_params[6])
    third_low = third_out.astype(jnp.bfloat16)
    pre_act = times_trans(third_low, up_rows)
    hidden_low = jax.nn.gelu(pre_act).astype(jnp.bfloat16)
    layer_out = (resid_two + project(hidden_low, down_rows)).astype(jnp.bfloat16)
    grad_out = cotangent.astype(jnp.float32)
    grad_down = weight_grad(hidden_low, cotangent)
    grad_hidden = times_trans(cotangent, down_rows)
    gelu_value, gelu_back = jax.vjp(jax.nn.gelu, pre_act)
    grad_pre_low = gelu_back(grad_hidden)[0].astype(jnp.bfloat16)
    grad_up = weight_grad(grad_pre_low, third_low)
    grad_third = project(grad_pre_low, up_rows)
    grad_norm_three, gain_three, shift_three = norm_backward(
        grad_third, third_normed, third_inv, norm_params[2]
    )
    grad_two = grad_out + grad_norm_three
    grad_cross_low = grad_two.astype(jnp.bfloat16)
    grad_cout = weight_grad(cross_low, grad_cross_low)
    grad_cross_att = (
        times_trans(grad_cross_low, c_output).astype(jnp.bfloat16).reshape(tok_rows, HEADS, HDIM)
    )
    caption_grad = jnp.where(
        slot_valid[:, :, None, None], grad_cross_att[pad_index], jnp.zeros((), jnp.bfloat16)
    )
    probs_cross = jnp.exp(cross_raw - cross_lse)
    probs_cross_low = probs_cross.astype(jnp.bfloat16)
    grad_cap_values = jnp.einsum(
        "chqk,cqhd->ckhd", probs_cross_low, caption_grad, preferred_element_type=jnp.float32
    )
    grad_cap_probs = jnp.einsum(
        "cqhd,ckhd->chqk", caption_grad, caption_values, preferred_element_type=jnp.float32
    )
    grad_cap_scores = (
        probs_cross
        * (grad_cap_probs - jnp.sum(grad_cap_probs * probs_cross, axis=-1, keepdims=True))
    ).astype(jnp.bfloat16)
    grad_cap_query = (
        jnp.einsum(
            "chqk,ckhd->cqhd", grad_cap_scores, caption_keys, preferred_element_type=jnp.float32
        )
        * score_scale
    )
    grad_cap_keys = (
        jnp.einsum(
            "chqk,cqhd->ckhd", grad_cap_scores, caption_query, preferred_element_type=jnp.float32
        )
        * score_scale
    )
    grad_cquery = grad_cap_query[segment, token_slot]
    grad_ckeys_low = (
        jnp.einsum("ci,ckhd->ikhd", caption_onehot, grad_cap_keys)
        .astype(jnp.bfloat16)
        .reshape(images_dev, patches, D)
    )
    grad_cvalues_low = (
        jnp.einsum("ci,ckhd->ikhd", caption_onehot, grad_cap_values)
        .astype(jnp.bfloat16)
        .reshape(images_dev, patches, D)
    )
    grad_ckey = jnp.einsum(
        "ipd,ipe->de", arrived, grad_ckeys_low, preferred_element_type=jnp.float32
    )
    grad_cvalue = jnp.einsum(
        "ipd,ipe->de", arrived, grad_cvalues_low, preferred_element_type=jnp.float32
    )
    grad_sent = jnp.einsum(
        "ipe,de->ipd", grad_ckeys_low, c_key, preferred_element_type=jnp.float32
    ) + jnp.einsum("ipe,de->ipd", grad_cvalues_low, c_value, preferred_element_type=jnp.float32)
    returned = from_partner(grad_sent.astype(jnp.bfloat16), "tower", 0)
    grad_images, gain_enc, shift_enc = norm_backward(
        returned.astype(jnp.float32), enc_normed, enc_inv, norm_params[3]
    )
    grad_cquery_low = grad_cquery.astype(jnp.bfloat16).reshape(tok_rows, D)
    grad_cq = weight_grad(second_low, grad_cquery_low)
    grad_second = times_trans(grad_cquery_low, c_query)
    grad_norm_two, gain_two, shift_two = norm_backward(
        grad_second, second_normed, second_inv, norm_params[1]
    )
    grad_one = grad_two + grad_norm_two
    grad_self_low = grad_one.astype(jnp.bfloat16)
    grad_wout = weight_grad(attended_low, grad_self_low)
    grad_att = (
        times_trans(grad_self_low, w_output).astype(jnp.bfloat16).reshape(tok_rows, HEADS, HDIM)
    )
    probs_again = jnp.exp(masked - self_lse)
    part_query, part_keys, part_values = attend_back(
        query, keys, values, probs_again, grad_att, score_scale
    )
    grad_q_low = part_query.astype(jnp.bfloat16).reshape(tok_rows, D)
    grad_k_low = part_keys.astype(jnp.bfloat16).reshape(tok_rows, D)
    grad_v_low = part_values.astype(jnp.bfloat16).reshape(tok_rows, D)
    grad_wq = weight_grad(first_low, grad_q_low)
    grad_wk = weight_grad(first_low, grad_k_low)
    grad_wv = weight_grad(first_low, grad_v_low)
    grad_first = (
        times_trans(grad_q_low, w_query)
        + times_trans(grad_k_low, w_key)
        + times_trans(grad_v_low, w_value)
    )
    grad_norm_one, gain_one, shift_one = norm_backward(
        grad_first, first_normed, first_inv, norm_params[0]
    )
    grad_tokens = grad_one + grad_norm_one
    logical_grads = jnp.concatenate(
        [
            grad_wq,
            grad_wk,
            grad_wv,
            grad_wout,
            grad_cq,
            grad_ckey,
            grad_cvalue,
            grad_cout,
            grad_up,
            grad_down,
        ],
        axis=0,
    )
    arranged = logical_grads.reshape(groups, group_rows, D)[owner_list].reshape(total_rows, D)
    reduced = lax.psum_scatter(arranged, ("tower", "dp"), scatter_dimension=0, tiled=True)
    norm_terms = jnp.stack(
        [gain_one, gain_two, gain_three, gain_enc, shift_one, shift_two, shift_three, shift_enc]
    )
    norm_grads = lax.psum(norm_terms, ("tower", "dp"))
    new_weights, new_first, new_second = adamw_update(
        master_weights, first_moments, second_moments, reduced, learn_rate, weight_decay
    )
    norm_new, norm_first_new, norm_second_new = adamw_update(
        norm_params, norm_first, norm_second, norm_grads, norm_rate, 0.0
    )
    return (
        layer_out,
        grad_tokens,
        grad_images,
        new_weights,
        new_first,
        new_second,
        new_weights.astype(jnp.bfloat16),
        norm_new,
        norm_first_new,
        norm_second_new,
    )


def solution(mesh):
    in_specs = (
        P(("tower", "dp"), None),
        P(("tower", "dp"), None),
        P(("tower", "dp"), None),
        P(("tower", "dp"), None),
        P(("tower", "dp"), None, None),
        P(("tower", "dp"), None),
        P(("tower", "dp"), None),
        P(("tower", "dp"), None),
        P(),
        P(),
        P(),
        P(),
    )
    out_specs = (
        P(("tower", "dp"), None),
        P(("tower", "dp"), None),
        P(("tower", "dp"), None, None),
        P(("tower", "dp"), None),
        P(("tower", "dp"), None),
        P(("tower", "dp"), None),
        P(("tower", "dp"), None),
        P(),
        P(),
        P(),
    )
    return jax.shard_map(
        per_device, mesh=mesh, in_specs=in_specs, out_specs=out_specs, check_vma=False
    )
```

profile of v0, /device:TPU:0, one launch (start us, length us, event | category | flops | bytes accessed | tf_op | source)
XLA Modules:
  0.0 1230.9 jit_solution(904814164243283533)
XLA Ops:
  33.0 10.8 select_select_fusion
  46.0 130.3 %all-gather.2.cloned.1.call-done = bf16[12288,768]{1,0:T(8,128)(2,1)} async-done(((bf16[384,768]{1,0:T(8,128)(2,1)}), bf16[12288,768]{1,0:T(8,128)(2,1)}) %all-gather.2.cloned.1.call-update) | async-done | bytes 18874384 | tf_op jit(solution)/shard_map/all_gather | solution.py:135
  176.3 14.8 %gather_fusion = bf16[64,192,768]{2,1,0:T(8,128)(2,1)} fusion(bf16[64,192,768]{2,1,0:T(8,128)(2,1)} %bitcast.177, s32[1024]{0:T(1024)S(1)} %pad_clamp_fusion.3), kind=kCustom, calls=%fused_computation | custom fusion | bytes 37748992 | tf_op jit(solution)/shard_map/gather | solution.py:139
  191.1 5.7 fusion.104
  196.9 10.4 fusion.103
  211.4 11.7 fusion.107
  223.1 11.8 fusion.6
  235.6 12.4 %fusion.72 = bf16[12,64,768]{2,1,0:T(8,128)(2,1)} fusion(bf16[768,12,64]{0,2,1:T(8,128)(2,1)S(1)} %bitcast.226, f32[12,768,768]{1,2,0:T(8,128)} %get-tuple-element.145, f32[12,768]{1,0:T(8,128)S(1)} %fusion.6, f32[12,768]{1,0:T(8,128)S(1)} %get-tuple-element.144), kind=kOutput, calls=%fused_computation.139 | convolution fusion | flops 927793152 | bytes 30744576 | tf_op jit(solution)/shard_map/hqk,khd->qhd/dot_general | solution.py:168
  248.0 6.7 convolution_convert_fusion.1
  254.7 5.9 copy.157
  277.2 9.1 copy.180
  295.3 11.7 gather_fusion.1
  307.0 11.7 gather_fusion.3
  318.7 24.5 %multiply_reduce_fusion.1 = (f32[24,12,64]{2,1,0:T(8,128)S(1)}, f32[24,12,64,576]{3,2,1,0:T(8,128)}) fusion(bf16[24,64,12,64]{1,3,2,0:T(8,128)(2,1)} %copy.180, bf16[24,576,12,64]{1,3,2,0:T(8,128)(2,1)} %gather_fusion.3), kind=kOutput, calls=%fused_computation.19 | convolution fusion | flops 1380169728 | bytes 66134016 | tf_op jit(solution)/shard_map/cqhd,ckhd->chqk/dot_general | solution.py:190
  343.2 20.2 %fusion.4 = f32[24,12,64]{2,1,0:T(8,128)S(1)} fusion(f32[24,12,64,576]{3,2,1,0:T(8,128)} %get-tuple-element.149, f32[24,12,64]{2,1,0:T(8,128)S(1)} %get-tuple-element.148), kind=kLoop, calls=%fused_computation.18 | loop fusion | flops 31832064 | bytes 42614784 | tf_op jit(solution)/shard_map/reduce_sum | solution.py:74
  363.5 26.0 %fusion.53 = bf16[24,64,12,64]{1,3,2,0:T(8,128)(2,1)} fusion(bf16[24,576,12,64]{1,3,2,0:T(8,128)(2,1)} %gather_fusion.1, f32[24,12,64,576]{3,2,1,0:T(8,128)} %get-tuple-element.149, f32[24,12,64]{2,1,0:T(8,128)S(1)} %fusion.4, f32[24,12,64]{2,1,0:T(8,128)S(1)} %get-tuple-element.148), kind=kOutput, calls=%fused_computation.84 | convolution fusion | flops 1401421824 | bytes 66207744 | tf_op jit(solution)/shard_map/chqk,ckhd->cqhd/dot_general | solution.py:196
  389.6 9.1 copy.162
  398.7 8.3 gather_fusion.4
  419.7 9.1 fusion.29
  428.8 5.8 fusion.111
  453.9 8.8 copy.204
  465.4 40.8 %multiply_reduce_fusion = (f32[24,12,64]{2,1,0:T(8,128)S(1)}, f32[24,12,64,576]{3,2,1,0:T(8,128)}) fusion(f32[24,12,64,576]{3,2,1,0:T(8,128)} %get-tuple-element.149, f32[24,12,64]{2,1,0:T(8,128)S(1)} %log_add_fusion, bf16[24,576,12,64]{1,3,2,0:T(8,128)(2,1)} %gather_fusion.1, bf16[24,64,12,64]{1,0,3,2:T(8,128)(2,1)S(1)} %broadcast_select_fusion), kind=kOutput, calls=%fused_computation.14 | convolution fusion | flops 1401403392 | bytes 108675072 | tf_op jit(solution)/shard_map/cqhd,ckhd->chqk/dot_general | solution.py:234
  506.2 37.7 %multiply_convert_fusion = bf16[24,12,64,576]{3,2,1,0:T(8,128)(2,1)} fusion(f32[24,12,64,576]{3,2,1,0:T(8,128)} %get-tuple-element.153, f32[24,12,64,576]{3,2,1,0:T(8,128)} %get-tuple-element.149, f32[24,12,64]{2,1,0:T(8,128)S(1)} %get-tuple-element.152, f32[24,12,64]{2,1,0:T(8,128)S(1)} %log_add_fusion), kind=kLoop, calls=%fused_computation.13 | loop fusion | flops 53084160 | bytes 106315776 | tf_op jit(solution)/shard_map/convert_element_type | solution.py:240
  544.0 18.8 %multiply_bitcast_fusion.1 = bf16[24,64,12,64]{1,3,2,0:T(8,128)(2,1)} fusion(bf16[24,576,12,64]{1,3,2,0:T(8,128)(2,1)} %gather_fusion.3, bf16[24,12,64,576]{3,2,1,0:T(8,128)(2,1)} %multiply_convert_fusion), kind=kOutput, calls=%fused_computation.57 | convolution fusion | flops 1361313792 | bytes 44826624 | tf_op jit(solution)/shard_map/chqk,ckhd->cqhd/dot_general | solution.py:242
  562.8 9.0 copy.171
  571.8 8.3 gather_fusion.6
  597.0 12.6 %fusion.69 = bf16[12,64,768]{2,1,0:T(8,128)(2,1)} fusion(bf16[768,12,64]{0,2,1:T(8,128)(2,1)S(1)} %bitcast.196, f32[12,768,768]{1,2,0:T(8,128)} %get-tuple-element.145, f32[12,768]{1,0:T(8,128)S(1)} %copy-done.50), kind=kOutput, calls=%fused_computation.138 | convolution fusion | flops 920715264 | bytes 30707712 | tf_op jit(solution)/shard_map/hqk,qhd->khd/dot_general | solution.py:80
  609.6 22.7 %multiply_reduce_fusion.2 = (f32[12,768]{1,0:T(8,128)}, f32[12,768,768]{1,2,0:T(8,128)}) fusion(f32[12,768,768]{1,2,0:T(8,128)} %get-tuple-element.145, f32[12,768]{1,0:T(8,128)} %log_add_fusion.1, bf16[768,12,64]{0,2,1:T(8,128)(2,1)S(1)} %bitcast.197, bf16[768,12,64]{0,2,1:T(8,128)(2,1)} %bitcast.227), kind=kOutput, calls=%fused_computation.22 | convolution fusion | flops 927194112 | bytes 59056128 | tf_op jit(solution)/shard_map/qhd,khd->hqk/dot_general | solution.py:83
  632.2 23.5 %multiply_convert_fusion.1 = bf16[12,768,768]{1,2,0:T(8,128)(2,1)} fusion(f32[12,768,768]{1,2,0:T(8,128)} %get-tuple-element.155, f32[12,768,768]{1,2,0:T(8,128)} %get-tuple-element.145, f32[12,768]{1,0:T(8,128)} %get-tuple-element.154, f32[12,768]{1,0:T(8,128)} %log_add_fusion.1), kind=kLoop, calls=%fused_computation.21 | loop fusion | flops 28311552 | bytes 70852608 | tf_op jit(solution)/shard_map/convert_element_type | solution.py:86
  655.8 8.7 multiply_convert_fusion.4
  664.5 10.5 multiply_convert_fusion.3
  674.9 20.5 %multiply_bitcast_fusion = bf16[24,576,12,64]{1,3,2,0:T(8,128)(2,1)} fusion(bf16[24,64,12,64]{1,3,2,0:T(8,128)(2,1)} %copy.180, bf16[24,12,64,576]{3,2,1,0:T(8,128)(2,1)} %multiply_convert_fusion), kind=kOutput, calls=%fused_computation.12 | convolution fusion | flops 1380188160 | bytes 44826624 | tf_op jit(solution)/shard_map/chqk,cqhd->ckhd/dot_general | solution.py:248
  695.4 26.1 %fusion.13 = bf16[24,576,12,64]{1,3,2,0:T(8,128)(2,1)} fusion(f32[24,12,64,576]{3,2,1,0:T(8,128)} %get-tuple-element.149, f32[24,12,64]{2,1,0:T(8,128)S(1)} %copy-done.28, bf16[24,64,12,64]{1,0,3,2:T(8,128)(2,1)} %copy-done.3), kind=kOutput, calls=%fused_computation.33 | convolution fusion | flops 1390804992 | bytes 66134016 | tf_op jit(solution)/shard_map/chqk,cqhd->ckhd/dot_general | solution.py:231
  721.5 28.9 %fusion.44 = bf16[4,576,12,64]{1,0,3,2:T(4,128)(2,1)} fusion(bf16[24,576,12,64]{1,3,2,0:T(8,128)(2,1)} %multiply_bitcast_fusion, s32[24]{0:T(128)S(1)} %bitcast.228), kind=kOutput, calls=%fused_computation.76 | convolution fusion | flops 84934752 | bytes 24772704 | tf_op jit(solution)/shard_map/ci,ckhd->ikhd/dot_general | solution.py:255
  750.4 8.0 copy.182
  758.4 28.8 %fusion.47 = bf16[4,576,12,64]{1,0,3,2:T(4,128)(2,1)} fusion(bf16[24,576,12,64]{1,3,2,0:T(8,128)(2,1)} %fusion.13, s32[24]{0:T(128)S(1)} %bitcast.229), kind=kOutput, calls=%fused_computation.77 | convolution fusion | flops 84934752 | bytes 24772704 | tf_op jit(solution)/shard_map/ci,ckhd->ikhd/dot_general | solution.py:260
  787.2 8.3 copy.185
  810.3 6.6 bitcast_dynamic-update-slice_fusion.1
  816.9 6.6 bitcast_dynamic-update-slice_fusion
  826.2 7.4 convolution_dynamic-update-slice_fusion.1
  833.6 7.8 convolution_dynamic-update-slice_fusion
  841.4 26.2 %gather_fusion.7 = f32[64,192,768]{2,1,0:T(8,128)} fusion(f32[64,192,768]{2,1,0:T(8,128)} %bitcast.80, s32[1024]{0:T(1024)} %get-tuple-element.161), kind=kCustom, calls=%fused_computation.7 | custom fusion | bytes 75497728 | tf_op jit(solution)/shard_map/gather | solution.py:323
  879.0 10.9 add_convert_fusion.1
  913.5 51.9 %collective-permute-done.1 = bf16[4,576,768]{2,1,0:T(8,128)(2,1)} collective-permute-done((bf16[4,576,768]{2,1,0:T(8,128)(2,1)}, bf16[4,576,768]{2,1,0:T(8,128)(2,1)}, u32[]{:S(2)}, u32[]{:S(2)}) %collective-permute-start.1) | collective-permute-done | bytes 3538976 | tf_op jit(solution)/shard_map/ppermute | solution.py:31
  965.5 5.9 fusion.43
  974.0 42.0 %psum.7 = f32[8,768]{1,0:T(8,128)} all-reduce(f32[8,768]{1,0:T(8,128)} %stack.35), channel_id=1, replica_groups=mesh['tower'=2,'dp'=16] {'tower','dp'}, use_global_device_ids=true, to_apply=%region_34.35 | all-reduce | flops 6144 | bytes 49152 | tf_op jit(solution)/shard_map/psum | solution.py:328
  1018.9 6.5 fusion.40
  1025.4 193.1 %reduce-scatter.2.cloned.1.call-done = f32[384,768]{1,0:T(8,128)} async-done(((f32[12288,768]{1,0:T(8,128)}), f32[384,768]{1,0:T(8,128)}) %reduce-scatter.2.cloned.1.call-update) | async-done | bytes 1179664 | tf_op jit(solution)/shard_map/reduce_scatter | solution.py:324
  (317 shorter events, 172.3 us)
Async XLA Ops:
  7.2 169.1 %all-gather.2.cloned.1.call-start = ((), (), s32[]{:S(2)}) async-start(), calls=%async_computation.1 | async-start | bytes 19464192 | tf_op jit(solution)/shard_map/all_gather | solution.py:135
  9.4 1209.1 %reduce-scatter.2.cloned.1.call-start = ((), (), s32[]{:S(2)}) async-start(), calls=%async_computation.2 | async-start | bytes 38928384 | tf_op jit(solution)/shard_map/reduce_scatter | solution.py:324
  11.1 198.9 %copy-start.72 = (f32[768]{0:T(1024)}, f32[768]{0:T(1024)S(1)}, u32[]{:S(2)}) copy-start(f32[768]{0:T(1024)S(1)} %get-tuple-element.82) | copy-start | bytes 9220
  11.1 252.3 %copy-start.68 = (f32[768]{0:T(1024)}, f32[768]{0:T(1024)S(1)}, u32[]{:S(2)}) copy-start(f32[768]{0:T(1024)S(1)} %get-tuple-element.78) | copy-start | bytes 9220
  11.1 252.3 %copy-start.81 = (f32[768]{0:T(1024)}, f32[768]{0:T(1024)S(1)}, u32[]{:S(2)}) copy-start(f32[768]{0:T(1024)S(1)} %get-tuple-element.77) | copy-start | bytes 9220
  17.6 14.6 %copy-start.85 = (s32[1,24]{1,0:T(1,128)S(1)}, s32[1,24]{1,0:T(1,128)}, u32[]{:S(2)}) copy-start(s32[1,24]{1,0:T(1,128)} %param.15) | copy-start | bytes 292
  17.7 230.3 %collective-permute-start = (bf16[4,576,768]{2,1,0:T(8,128)(2,1)}, bf16[4,576,768]{2,1,0:T(8,128)(2,1)}, u32[]{:S(2)}, u32[]{:S(2)}) collective-permute-start(bf16[4,576,768]{2,1,0:T(8,128)(2,1)} %fusion.38), channel_id=1, source_target_pairs={{0,16},{16,0},{1,17},{17,1},{2,18},{18,2},{3,19},{19,3},{4,20},{20... | collective-permute-start | bytes 10616840 | tf_op jit(solution)/shard_map/ppermute | solution.py:31
  22.2 238.4 %copy-start.16 = (bf16[768,768]{0,1:T(8,128)(2,1)}, bf16[768,768]{0,1:T(8,128)(2,1)S(1)}, u32[]{:S(2)}) copy-start(bf16[768,768]{0,1:T(8,128)(2,1)S(1)} %copy.154) | copy-start | bytes 3538948
  32.2 239.4 %copy-start.54 = (s32[2048]{0:T(1024)}, s32[2048]{0:T(1024)S(1)}, u32[]{:S(2)}) copy-start(s32[2048]{0:T(1024)S(1)} %pad_clamp_fusion) | copy-start | bytes 24580
  44.6 165.4 %copy-start.64 = (f32[768]{0:T(1024)}, f32[768]{0:T(1024)S(1)}, u32[]{:S(2)}) copy-start(f32[768]{0:T(1024)S(1)} %broadcast_multiply_fusion.13) | copy-start | bytes 9220
  45.6 164.4 %copy-start.75 = (f32[768]{0:T(1024)}, f32[768]{0:T(1024)S(1)}, u32[]{:S(2)}) copy-start(f32[768]{0:T(1024)S(1)} %add_rsqrt_fusion.3) | copy-start | bytes 9220
  196.8 10.5 copy-start.29
  196.8 11.8 copy-start.33
  196.8 13.2 %copy-start.31 = (bf16[4,192,768]{2,1,0:T(8,128)(2,1)}, bf16[4,192,768]{2,1,0:T(8,128)(2,1)S(1)}, u32[]{:S(2)}) copy-start(bf16[4,192,768]{2,1,0:T(8,128)(2,1)S(1)} %get-tuple-element.115) | copy-start | bytes 3538948
  196.9 51.1 %copy-start.34 = (bf16[4,192,768]{2,1,0:T(8,128)(2,1)}, bf16[4,192,768]{2,1,0:T(8,128)(2,1)S(1)}, u32[]{:S(2)}) copy-start(bf16[4,192,768]{2,1,0:T(8,128)(2,1)S(1)} %get-tuple-element.113) | copy-start | bytes 3538948
  196.9 63.7 %copy-start.36 = (bf16[4,192,768]{2,1,0:T(8,128)(2,1)}, bf16[4,192,768]{2,1,0:T(8,128)(2,1)S(1)}, u32[]{:S(2)}) copy-start(bf16[4,192,768]{2,1,0:T(8,128)(2,1)S(1)} %get-tuple-element.114) | copy-start | bytes 3538948
  196.9 10.4 copy-start.83
  208.6 26.9 %copy-start.49 = (bf16[768,768]{0,1:T(8,128)(2,1)}, bf16[768,768]{0,1:T(8,128)(2,1)S(1)}, u32[]{:S(2)}) copy-start(bf16[768,768]{0,1:T(8,128)(2,1)S(1)} %convolution_convert_fusion.7) | copy-start | bytes 3538948
  211.4 11.8 copy-start.18
  363.5 142.8 %copy-start.27 = (f32[24,12,64]{2,1,0:T(8,128)}, f32[24,12,64]{2,1,0:T(8,128)S(1)}, u32[]{:S(2)}) copy-start(f32[24,12,64]{2,1,0:T(8,128)S(1)} %log_add_fusion) | copy-start | bytes 221188
  389.5 9.1 copy-start
  410.0 9.7 slice-start
  413.7 27.2 %copy-start.4 = (f32[768,768]{0,1:T(8,128)}, f32[768,768]{0,1:T(8,128)S(1)}, u32[]{:S(2)}) copy-start(f32[768,768]{0,1:T(8,128)S(1)} %get-tuple-element.151) | copy-start | bytes 7077892
  413.7 27.2 %copy-start.56 = (f32[768]{0:T(1024)}, f32[768]{0:T(1024)S(1)}, u32[]{:S(2)}) copy-start(f32[768]{0:T(1024)S(1)} %broadcast_multiply_fusion.11) | copy-start | bytes 9220
  414.0 26.9 %copy-start.66 = (f32[768]{0:T(1024)}, f32[768]{0:T(1024)S(1)}, u32[]{:S(2)}) copy-start(f32[768]{0:T(1024)S(1)} %add_rsqrt_fusion.1) | copy-start | bytes 9220
  419.6 9.1 copy-start.89
  453.9 8.8 copy-start.78
  465.4 40.8 %copy-start.3 = (bf16[24,64,12,64]{1,0,3,2:T(8,128)(2,1)}, bf16[24,64,12,64]{1,0,3,2:T(8,128)(2,1)S(1)}, u32[]{:S(2)}) copy-start(bf16[24,64,12,64]{1,0,3,2:T(8,128)(2,1)S(1)} %broadcast_select_fusion) | copy-start | bytes 7077892
  632.2 23.5 %copy-start.19 = (bf16[768,768]{0,1:T(8,128)(2,1)S(1)}, bf16[768,768]{0,1:T(8,128)(2,1)}, u32[]{:S(2)}) copy-start(bf16[768,768]{0,1:T(8,128)(2,1)} %copy-done.18) | copy-start | bytes 3538948
  655.8 8.7 copy-start.21
  674.9 20.5 %copy-start.28 = (f32[24,12,64]{2,1,0:T(8,128)S(1)}, f32[24,12,64]{2,1,0:T(8,128)}, u32[]{:S(2)}) copy-start(f32[24,12,64]{2,1,0:T(8,128)} %copy-done.27) | copy-start | bytes 221188
  695.4 26.1 %copy-start.86 = (s32[1,24]{1,0:T(1,128)S(1)}, s32[1,24]{1,0:T(1,128)}, u32[]{:S(2)}) copy-start(s32[1,24]{1,0:T(1,128)} %param.15) | copy-start | bytes 292
  787.2 8.3 copy-start.17
  787.2 8.3 copy-start.65
  810.3 6.6 copy-start.25
  810.3 15.8 %slice-start.9 = ((s8[4718592]{0:T(1024)(128)(4,1)}), s8[4194304]{0:T(1024)(128)(4,1)S(1)}, s32[]{:S(2)}) async-start(s8[4718592]{0:T(1024)(128)(4,1)} %bitcast.234), calls=%async_computation.12 | async-start | bytes 8388608
  816.9 6.6 copy-start.14
  816.9 6.6 copy-start.23
  816.9 9.2 slice-start.10
  823.6 10.0 slice-start.6
  826.2 7.4 copy-start.46
  826.2 7.4 slice-start.7
  826.2 7.4 slice-start.8
  867.7 11.3 slice-start.2
  877.9 87.5 %collective-permute-start.1 = (bf16[4,576,768]{2,1,0:T(8,128)(2,1)}, bf16[4,576,768]{2,1,0:T(8,128)(2,1)}, u32[]{:S(2)}, u32[]{:S(2)}) collective-permute-start(bf16[4,576,768]{2,1,0:T(8,128)(2,1)} %add_convert_fusion), channel_id=1, source_target_pairs={{0,16},{16,0},{1,17},{17,1},{2,18},{18,2},{3,19},{19,3},{4,20},{20... | collective-permute-start | bytes 10616840 | tf_op jit(solution)/shard_map/ppermute | solution.py:31
  902.4 63.1 %copy-start.2 = (bf16[4,576,768]{2,1,0:T(8,128)(2,1)S(1)}, bf16[4,576,768]{2,1,0:T(8,128)(2,1)}, u32[]{:S(2)}) copy-start(bf16[4,576,768]{2,1,0:T(8,128)(2,1)} %param.16) | copy-start | bytes 10616836
  902.4 63.1 %copy-start.52 = (f32[4,576]{1,0:T(4,128)S(1)}, f32[4,576]{1,0:T(4,128)}, u32[]{:S(2)}) copy-start(f32[4,576]{1,0:T(4,128)} %copy-done.51) | copy-start | bytes 27652
  902.4 63.1 %copy-start.59 = (f32[768]{0:T(1024)S(1)}, f32[768]{0:T(1024)}, u32[]{:S(2)}) copy-start(f32[768]{0:T(1024)} %copy-done.58) | copy-start | bytes 9220
  (58 other events, 189.2 us)
Sparse Core Ops, SparseCore 0:
  11.5 164.7 all-gather.1
  867.8 350.6 reduce-scatter.1
where the time goes:
time: 1240 us; the launch traced here: 1230 us
  matrix products  418 us (34%)
  waiting for transfers between devices  375 us (30%)
  local copies, waits for them, and re-layouts  219 us (18%)
  other arithmetic  157 us (13%)
  blocking collectives  42 us (3%)
  between operations  15.5 us (1%)
    reduce_scatter x1, waiting for transfers between devices, per_device(): lax.psum_scatter(arranged, ('tower', 'dp'), scatter_dimension=0, tiled=True)  193 us
    all_gather x1, waiting for transfers between devices, per_device(): lax.all_gather(master_weights.astype(jnp.bfloat16), ('tower', 'dp'), axis...  130 us
    ppermute x2, waiting for transfers between devices, from_partner(): return lax.ppermute(block, axis, route)  51.9 us
    psum x1, blocking collectives, per_device(): norm_grads = lax.psum(norm_terms, ('tower', 'dp'))  42 us
    dot_general x1, matrix products, per_device(): jnp.einsum('cqhd,ckhd->chqk', caption_grad, caption_values, preferred_ele...  40.8 us
    convert_element_type x1, other arithmetic, per_device(): grad_cap_scores = (probs_cross * (grad_cap_probs - jnp.sum(grad_cap_probs...  37.7 us
    dot_general x8, matrix products, weight_grad(): lax.dot_general(left, right, (((0,), (0,)), ((), ())), preferred_element_...  32.4 us
    reduce_sum x2, other arithmetic, row_softmax(): row_total = jnp.sum(exponent, axis=-1, keepdims=True)  32 us
  transfers between devices with their start and end apart: 4, of which 3 were waited for; matrix products, arithmetic and copies ran while one was open for 14% of the time, Pallas kernels for 0%

commit v1 on v0

v1 whole, which is shorter than its diff:
```python
import functools

import jax
import jax.numpy as jnp
from jax import lax
from jax.experimental import pallas as pl
from jax.experimental.pallas import tpu as pltpu
from jax.sharding import PartitionSpec as P

D = 768
HEADS = 12
HDIM = 64
FF = 3072
STEP = 5
PAIRS = HEADS // 2
LANES = 2 * HDIM
QB = 128
GROUP = 192
PER = D // GROUP
SCALE = HDIM ** (-0.5)

beta_one = 0.5
beta_two = 0.6
learn_rate = 0.03
norm_rate = 0.4
weight_decay = 0.01
epsilon = 1e-08
norm_eps = 1e-05
masked_score = -1000000000.0

W_Q, W_K, W_V, W_O, C_Q, C_K, C_V, C_O, UP, DOWN = 0, 1, 2, 3, 4, 5, 6, 7, 8, 12

BF = jnp.bfloat16
F32 = jnp.float32
VM = pl.BlockSpec(memory_space=pltpu.VMEM)
SM = pl.BlockSpec(memory_space=pltpu.SMEM)
ANY = pl.BlockSpec(memory_space=pl.ANY)
VLIM = 58 * 2**20


def nn(a, b):
    return lax.dot_general(a, b, (((1,), (0,)), ((), ())), preferred_element_type=F32)


def nt(a, b):
    return lax.dot_general(a, b, (((1,), (1,)), ((), ())), preferred_element_type=F32)


def tn(a, b):
    return lax.dot_general(a, b, (((0,), (0,)), ((), ())), preferred_element_type=F32)


def blk(i, size=QB):
    return pl.ds(pl.multiple_of(i * size, size), size)


def lanes(p):
    return slice(p * LANES, (p + 1) * LANES)


def normalise(x):
    centred = x - jnp.mean(x, axis=-1, keepdims=True)
    inv = lax.rsqrt(jnp.mean(centred * centred, axis=-1, keepdims=True) + norm_eps)
    return centred * inv, inv


def norm_back(grad, normed, inv, gain):
    gn = grad * gain
    m1 = jnp.mean(gn, axis=-1, keepdims=True)
    m2 = jnp.mean(gn * normed, axis=-1, keepdims=True)
    return inv * (gn - m1 - normed * m2)


def head_masks():
    low = (lax.broadcasted_iota(jnp.int32, (1, LANES), 1) < HDIM).astype(F32)
    return low.astype(BF), (1.0 - low).astype(BF)


def two_heads(x, masks):
    return jnp.concatenate([x * masks[0], x * masks[1]], axis=0)


def merge_heads(both):
    return jnp.concatenate([both[:HDIM, :QB], both[HDIM:, QB:]], axis=0)


def weight_copies(slots, inv, buf, sem, matrix, slot):
    return [
        pltpu.make_async_copy(
            slots.at[inv[matrix * PER + j]], buf.at[slot, pl.ds(j * GROUP, GROUP)], sem.at[slot, j]
        )
        for j in range(PER)
    ]


def grad_copies(grads, inv, buf, sem, matrix, slot):
    return [
        pltpu.make_async_copy(
            buf.at[slot, pl.ds(j * GROUP, GROUP)], grads.at[inv[matrix * PER + j]], sem.at[slot, j]
        )
        for j in range(PER)
    ]


def start(copies):
    for copy in copies:
        copy.start()


def wait(copies):
    for copy in copies:
        copy.wait()


def causal_mask(starts, b):
    query = lax.broadcasted_iota(jnp.int32, (1, QB), 1) + b * QB
    first = jnp.zeros((1, QB), jnp.int32)
    for c in range(starts.shape[0]):
        first = jnp.maximum(first, jnp.where(query >= starts[c], starts[c], 0))
    key = lax.broadcasted_iota(jnp.int32, (2 * QB, QB), 0) + (b - 1) * QB
    allowed = (key >= first) & (key <= query)
    return jnp.concatenate([allowed, allowed], axis=1)


def column_softmax(scores):
    top = jnp.max(scores, axis=0, keepdims=True)
    exponent = jnp.exp(scores - top)
    return exponent, 1.0 / jnp.sum(exponent, axis=0, keepdims=True)


def self_forward(
    inv, starts, x, norms, slots, q_o, k_o, v_o, att_o, r1_o, cq_o, wbuf, low, kpad, vpad, wsem
):
    rows = x.shape[0]
    loads = [weight_copies(slots, inv, wbuf, wsem, m, m) for m in range(5)]
    for load in loads:
        start(load)
    masks = head_masks()

    def norm_one(i, _):
        normed, _i = normalise(x[blk(i), :].astype(F32))
        low[blk(i), :] = (normed * norms[0:1, :] + norms[4:5, :]).astype(BF)
        return 0

    lax.fori_loop(0, rows // QB, norm_one, 0)
    kpad[pl.ds(0, QB), :] = jnp.zeros((QB, D), BF)
    vpad[pl.ds(0, QB), :] = jnp.zeros((QB, D), BF)
    wait(loads[0])
    q_o[...] = (nn(low[...], wbuf[0]) * SCALE).astype(BF)
    wait(loads[1])
    kpad[pl.ds(QB, rows), :] = nn(low[...], wbuf[1]).astype(BF)
    wait(loads[2])
    vpad[pl.ds(QB, rows), :] = nn(low[...], wbuf[2]).astype(BF)
    k_o[...] = kpad[pl.ds(QB, rows), :]
    v_o[...] = vpad[pl.ds(QB, rows), :]

    def attend(b, _):
        allowed = causal_mask(starts, b)
        for p in range(PAIRS):
            q2 = two_heads(q_o[blk(b), lanes(p)], masks)
            keys = kpad[pl.ds(pl.multiple_of(b * QB, QB), 2 * QB), lanes(p)]
            vals = vpad[pl.ds(pl.multiple_of(b * QB, QB), 2 * QB), lanes(p)]
            scores = jnp.where(allowed, nt(keys, q2), masked_score)
            exponent, scale = column_softmax(scores)
            out = tn(vals, (exponent * scale).astype(BF))
            att_o[blk(b), lanes(p)] = merge_heads(out).T.astype(BF)
        return 0

    lax.fori_loop(0, rows // QB, attend, 0)
    wait(loads[3])
    r1_o[...] = x[...].astype(F32) + nn(att_o[...], wbuf[3])

    def norm_two(i, _):
        normed, _i = normalise(r1_o[blk(i), :])
        low[blk(i), :] = (normed * norms[1:2, :] + norms[5:6, :]).astype(BF)
        return 0

    lax.fori_loop(0, rows // QB, norm_two, 0)
    wait(loads[4])
    cq_o[...] = (nn(low[...], wbuf[4]) * SCALE).astype(BF)


def call(body, out_shape, in_specs, out_specs, scratch, aliases=None, effects=False):
    return pl.pallas_call(
        body,
        out_shape=out_shape,
        in_specs=in_specs,
        out_specs=out_specs,
        scratch_shapes=scratch,
        input_output_aliases=aliases or {},
        compiler_params=pltpu.CompilerParams(vmem_limit_bytes=VLIM, has_side_effects=effects),
    )


def run_self_forward(inv, starts, x, norms, slots):
    rows = x.shape[0]
    one = jax.ShapeDtypeStruct((rows, D), BF)
    return call(
        self_forward,
        (one, one, one, one, jax.ShapeDtypeStruct((rows, D), F32), one),
        [SM, SM, VM, VM, ANY],
        (VM,) * 6,
        [
            pltpu.VMEM((5, D, D), BF),
            pltpu.VMEM((rows, D), BF),
            pltpu.VMEM((rows + QB, D), BF),
            pltpu.VMEM((rows + QB, D), BF),
            pltpu.SemaphoreType.DMA((5, PER)),
        ],
    )(inv, starts, x, norms, slots)


def image_blocks(bounds, i):
    low, high = bounds[i], bounds[i + 1]
    first = low // QB
    last = jnp.where(high > low, (high + QB - 1) // QB, first)
    return low, high, first, last


def cross_forward(
    images, inv, bounds, enc, cq, r1, slots, k_o, v_o, cross_o, r2_o, wbuf, acc, wsem
):
    patches = enc.shape[0] // images
    loads = [weight_copies(slots, inv, wbuf, wsem, m, i) for i, m in enumerate((C_K, C_V, C_O))]
    for load in loads:
        start(load)
    masks = head_masks()
    cross_o[...] = jnp.zeros_like(cross_o)
    for i, out in ((0, k_o), (1, v_o)):
        wait(loads[i])

        def project(c, _, i=i, out=out):
            out[blk(c, D), :] = nn(enc[blk(c, D), :], wbuf[i]).astype(BF)
            return 0

        lax.fori_loop(0, enc.shape[0] // D, project, 0)

    def image(i, _):
        low, high, first, last = image_blocks(bounds, i)

        def attend(b, _):
            token = lax.broadcasted_iota(jnp.int32, (1, QB), 1) + b * QB
            here = ((token >= low) & (token < high)).astype(F32)
            here = jnp.concatenate([here, here], axis=1)
            for p in range(PAIRS):
                q2 = two_heads(cq[blk(b), lanes(p)], masks)
                keys = k_o[blk_of(i, patches), lanes(p)]
                vals = v_o[blk_of(i, patches), lanes(p)]
                exponent, scale = column_softmax(nt(keys, q2))
                out = tn(vals, exponent.astype(BF)) * (scale * here)
                acc[blk(b), lanes(p)] += merge_heads(out).T
            return 0

        lax.fori_loop(first, last, attend, 0)
        return 0

    acc[...] = jnp.zeros_like(acc)
    lax.fori_loop(0, images, image, 0)
    cross_o[...] = acc[...].astype(BF)
    wait(loads[2])
    r2_o[...] = r1[...] + nn(cross_o[...], wbuf[2])


def blk_of(i, size):
    return pl.ds(pl.multiple_of(i * size, 64), size)


def run_cross_forward(images, inv, bounds, enc, cq, r1, slots):
    rows = cq.shape[0]
    kv = jax.ShapeDtypeStruct(enc.shape, BF)
    return call(
        functools.partial(cross_forward, images),
        (kv, kv, jax.ShapeDtypeStruct((rows, D), BF), jax.ShapeDtypeStruct((rows, D), F32)),
        [SM, SM, VM, VM, VM, ANY],
        (VM,) * 4,
        [
            pltpu.VMEM((3, D, D), BF),
            pltpu.VMEM((rows, D), F32),
            pltpu.SemaphoreType.DMA((3, PER)),
        ],
    )(inv, bounds, enc, cq, r1, slots)


GELU_A = 0.7978845608028654
GELU_B = GELU_A * 0.044715


def feed_forward(
    inv, r2, cot, norms, slots, out_o, g2_o, ng_o, grads,
    wup, wdown, third, pre, gh, hid, gpre, acc, gthird, gup, gdown, usem, dsem, gusem, gdsem,
):
    rows = r2.shape[0]
    chunks = FF // D

    def loads(c, slot):
        return weight_copies(slots, inv, wup, usem, UP + c, slot) + weight_copies(
            slots, inv, wdown, dsem, DOWN + c, slot
        )

    def stores(c, slot):
        return grad_copies(grads, inv, gup, gusem, UP + c, slot) + grad_copies(
            grads, inv, gdown, gdsem, DOWN + c, slot
        )

    start(loads(0, 0))

    def norm_three(i, _):
        normed, _i = normalise(r2[blk(i), :])
        third[blk(i), :] = (normed * norms[2:3, :] + norms[6:7, :]).astype(BF)
        return 0

    lax.fori_loop(0, rows // QB, norm_three, 0)
    acc[...] = r2[...]
    gthird[...] = jnp.zeros_like(gthird)

    def chunk(c, _):
        slot = c % 2

        @pl.when(c + 1 < chunks)
        def _():
            start(loads(c + 1, 1 - slot))

        wait(loads(c, slot))
        pre[...] = nt(third[...], wup[slot])
        gh[...] = nt(cot[...], wdown[slot])

        def gelu(i, _):
            x = pre[blk(i, 64), :]
            x2 = x * x
            t = jnp.tanh(x * (GELU_A + GELU_B * x2))
            half = 0.5 + 0.5 * t
            value = x * half
            hid[blk(i, 64), :] = value.astype(BF)
            slope = half + value * (1.0 - t) * (GELU_A + 3.0 * GELU_B * x2)
            gpre[blk(i, 64), :] = (gh[blk(i, 64), :] * slope).astype(BF)
            return 0

        lax.fori_loop(0, rows // 64, gelu, 0)

        @pl.when(c >= 2)
        def _():
            wait(stores(c - 2, slot))

        acc[...] += nn(hid[...], wdown[slot])
        gdown[slot] = tn(hid[...], cot[...]).astype(BF)
        gup[slot] = tn(gpre[...], third[...]).astype(BF)
        start(stores(c, slot))
        gthird[...] += nn(gpre[...], wup[slot])
        return 0

    lax.fori_loop(0, chunks, chunk, 0)
    out_o[...] = acc[...].astype(BF)
    ng_o[...] = jnp.zeros_like(ng_o)

    def back(i, _):
        normed, inv_std = normalise(r2[blk(i), :])
        grad = gthird[blk(i), :]
        ng_o[0:1, :] += jnp.sum(grad * normed, axis=0, keepdims=True)
        ng_o[1:2, :] += jnp.sum(grad, axis=0, keepdims=True)
        g2_o[blk(i), :] = cot[blk(i), :].astype(F32) + norm_back(
            grad, normed, inv_std, norms[2:3, :]
        )
        return 0

    lax.fori_loop(0, rows // QB, back, 0)
    for c in range(chunks - 2, chunks):
        wait(stores(c, c % 2))


def run_feed_forward(inv, r2, cot, norms, slots):
    rows = r2.shape[0]
    big = pltpu.VMEM((rows, D), F32)
    low = pltpu.VMEM((rows, D), BF)
    two = pltpu.VMEM((2, D, D), BF)
    sem = pltpu.SemaphoreType.DMA((2, PER))
    return call(
        feed_forward,
        (
            jax.ShapeDtypeStruct((rows, D), BF),
            jax.ShapeDtypeStruct((rows, D), F32),
            jax.ShapeDtypeStruct((2, D), F32),
            jax.ShapeDtypeStruct(slots.shape, BF),
        ),
        [SM, VM, VM, VM, ANY],
        (VM, VM, VM, ANY),
        [two, two, low, big, big, low, low, big, big, two, two, sem, sem, sem, sem],
    )(inv, r2, cot, norms, slots)


def cross_backward(
    images, inv, bounds, g2, cross, k, v, cq, r1, enc, img, norms, slots, grads_in,
    g1_o, gi_o, ng_o, grads,
    wbuf, gbuf, gca, dq, acck, accv, dk, dv, big, wsem, gsem,
):
    rows = g2.shape[0]
    patches = enc.shape[0] // images
    names = (C_O, C_Q, C_K, C_V)
    loads = [weight_copies(slots, inv, wbuf, wsem, m, i) for i, m in enumerate(names)]
    stores = [grad_copies(grads, inv, gbuf, gsem, m, i) for i, m in enumerate(names)]
    for load in loads:
        start(load)
    masks = head_masks()
    ng_o[...] = jnp.zeros_like(ng_o)
    low = dq
    low[...] = g2[...].astype(BF)
    gbuf[0] = tn(cross[...], low[...]).astype(BF)
    start(stores[0])
    wait(loads[0])
    gca[...] = nt(low[...], wbuf[0]).astype(BF)
    dq[...] = jnp.zeros_like(dq)

    def image(i, _):
        first_row, end_row, first, last = image_blocks(bounds, i)
        acck[...] = jnp.zeros_like(acck)
        accv[...] = jnp.zeros_like(accv)

        def attend(b, _):
            token = lax.broadcasted_iota(jnp.int32, (QB, LANES), 0) + b * QB
            here = ((token >= first_row) & (token < end_row)).astype(F32).astype(BF)
            for p in range(PAIRS):
                q2 = two_heads(cq[blk(b), lanes(p)], masks)
                go2 = two_heads(gca[blk(b), lanes(p)] * here, masks)
                keys = k[blk_of(i, patches), lanes(p)]
                vals = v[blk_of(i, patches), lanes(p)]
                exponent, scale = column_softmax(nt(keys, q2))
                probs = exponent * scale
                accv[:, lanes(p)] += nn(probs.astype(BF), go2)
                gp = nt(vals, go2)
                gs = probs * (gp - jnp.sum(gp * probs, axis=0, keepdims=True))
                gs = gs.astype(BF)
                acck[:, lanes(p)] += nn(gs, q2)
                gq = merge_heads(tn(keys, gs)).T * SCALE
                dq[blk(b), lanes(p)] += gq.astype(BF)
            return 0

        lax.fori_loop(first, last, attend, 0)
        dk[blk_of(i, patches), :] = acck[...].astype(BF)
        dv[blk_of(i, patches), :] = accv[...].astype(BF)
        return 0

    lax.fori_loop(0, images, image, 0)
    for slot, grad in ((2, dk), (3, dv)):
        big[...] = jnp.zeros_like(big)

        def gather(c, _, grad=grad):
            big[...] += tn(enc[blk(c, D), :], grad[blk(c, D), :])
            return 0

        lax.fori_loop(0, enc.shape[0] // D, gather, 0)
        gbuf[slot] = big[...].astype(BF)
        start(stores[slot])
    wait(loads[2])
    wait(loads[3])

    def encoder(c, _):
        sent = nt(dk[blk(c, D), :], wbuf[2]) + nt(dv[blk(c, D), :], wbuf[3])
        big[...] = sent

        def back(j, _):
            rows_j = pl.ds(pl.multiple_of(c * D + j * QB, QB), QB)
            normed, inv_std = normalise(img[rows_j, :].astype(F32))
            grad = big[blk(j), :].astype(BF).astype(F32)
            ng_o[2:3, :] += jnp.sum(grad * normed, axis=0, keepdims=True)
            ng_o[3:4, :] += jnp.sum(grad, axis=0, keepdims=True)
            gi_o[rows_j, :] = norm_back(grad, normed, inv_std, norms[3:4, :])
            return 0

        lax.fori_loop(0, D // QB, back, 0)
        return 0

    lax.fori_loop(0, enc.shape[0] // D, encoder, 0)

    def norm_two(i, _):
        normed, _i = normalise(r1[blk(i), :])
        gca[blk(i), :] = (normed * norms[1:2, :] + norms[5:6, :]).astype(BF)
        return 0

    lax.fori_loop(0, rows // QB, norm_two, 0)
    gbuf[1] = tn(gca[...], dq[...]).astype(BF)
    start(stores[1])
    wait(loads[1])
    big[...] = nt(dq[...], wbuf[1])

    def back_two(i, _):
        normed, inv_std = normalise(r1[blk(i), :])
        grad = big[blk(i), :]
        ng_o[0:1, :] += jnp.sum(grad * normed, axis=0, keepdims=True)
        ng_o[1:2, :] += jnp.sum(grad, axis=0, keepdims=True)
        g1_o[blk(i), :] = g2[blk(i), :] + norm_back(grad, normed, inv_std, norms[1:2, :])
        return 0

    lax.fori_loop(0, rows // QB, back_two, 0)
    for store in stores:
        wait(store)


def run_cross_backward(images, inv, bounds, g2, cross, k, v, cq, r1, enc, img, norms, slots, grads):
    rows = g2.shape[0]
    patches = enc.shape[0] // images
    four = pltpu.VMEM((4, D, D), BF)
    low = pltpu.VMEM((rows, D), BF)
    part = pltpu.VMEM((patches, D), F32)
    wide = pltpu.VMEM(enc.shape, BF)
    sem = pltpu.SemaphoreType.DMA((4, PER))
    return call(
        functools.partial(cross_backward, images),
        (
            jax.ShapeDtypeStruct((rows, D), F32),
            jax.ShapeDtypeStruct(enc.shape, F32),
            jax.ShapeDtypeStruct((4, D), F32),
            jax.ShapeDtypeStruct(slots.shape, BF),
        ),
        [SM, SM] + [VM] * 9 + [ANY, ANY],
        (VM, VM, VM, ANY),
        [four, four, low, low, part, part, wide, wide, pltpu.VMEM((D, D), F32), sem, sem],
        aliases={12: 3},
    )(inv, bounds, g2, cross, k, v, cq, r1, enc, img, norms, slots, grads)


def self_backward(
    inv, starts, g1, x, q, k, v, att, norms, slots, grads_in,
    gt_o, ng_o, grads,
    wbuf, gbuf, ga, dq, kpad, vpad, acck, accv, dk, dv, big, wsem, gsem,
):
    rows = g1.shape[0]
    names = (W_O, W_Q, W_K, W_V)
    loads = [weight_copies(slots, inv, wbuf, wsem, m, i) for i, m in enumerate(names)]
    stores = [grad_copies(grads, inv, gbuf, gsem, m, i) for i, m in enumerate(names)]
    for load in loads:
        start(load)
    masks = head_masks()
    ng_o[...] = jnp.zeros_like(ng_o)
    low = dq
    low[...] = g1[...].astype(BF)
    gbuf[0] = tn(att[...], low[...]).astype(BF)
    start(stores[0])
    wait(loads[0])
    ga[...] = nt(low[...], wbuf[0]).astype(BF)
    kpad[pl.ds(0, QB), :] = jnp.zeros((QB, D), BF)
    vpad[pl.ds(0, QB), :] = jnp.zeros((QB, D), BF)
    kpad[pl.ds(QB, rows), :] = k[...]
    vpad[pl.ds(QB, rows), :] = v[...]
    acck[...] = jnp.zeros_like(acck)
    accv[...] = jnp.zeros_like(accv)

    def attend(b, _):
        allowed = causal_mask(starts, b)
        span = pl.ds(pl.multiple_of(b * QB, QB), 2 * QB)
        for p in range(PAIRS):
            q2 = two_heads(q[blk(b), lanes(p)], masks)
            go2 = two_heads(ga[blk(b), lanes(p)], masks)
            keys = kpad[span, lanes(p)]
            vals = vpad[span, lanes(p)]
            scores = jnp.where(allowed, nt(keys, q2), masked_score)
            exponent, scale = column_softmax(scores)
            probs = exponent * scale
            accv[span, lanes(p)] += nn(probs.astype(BF), go2)
            gp = nt(vals, go2)
            gs = probs * (gp - jnp.sum(gp * probs, axis=0, keepdims=True))
            gs = gs.astype(BF)
            acck[span, lanes(p)] += nn(gs, q2)
            dq[blk(b), lanes(p)] = (merge_heads(tn(keys, gs)).T * SCALE).astype(BF)
        return 0

    lax.fori_loop(0, rows // QB, attend, 0)
    dk[...] = acck[pl.ds(QB, rows), :].astype(BF)
    dv[...] = accv[pl.ds(QB, rows), :].astype(BF)

    def norm_one(i, _):
        normed, _i = normalise(x[blk(i), :].astype(F32))
        ga[blk(i), :] = (normed * norms[0:1, :] + norms[4:5, :]).astype(BF)
        return 0

    lax.fori_loop(0, rows // QB, norm_one, 0)
    for slot, grad in ((1, dq), (2, dk), (3, dv)):
        gbuf[slot] = tn(ga[...], grad[...]).astype(BF)
        start(stores[slot])
    wait(loads[1])
    big[...] = nt(dq[...], wbuf[1])
    wait(loads[2])
    big[...] += nt(dk[...], wbuf[2])
    wait(loads[3])
    big[...] += nt(dv[...], wbuf[3])

    def back_one(i, _):
        normed, inv_std = normalise(x[blk(i), :].astype(F32))
        grad = big[blk(i), :]
        ng_o[0:1, :] += jnp.sum(grad * normed, axis=0, keepdims=True)
        ng_o[1:2, :] += jnp.sum(grad, axis=0, keepdims=True)
        gt_o[blk(i), :] = (g1[blk(i), :] + norm_back(grad, normed, inv_std, norms[0:1, :])).astype(
            BF
        )
        return 0

    lax.fori_loop(0, rows // QB, back_one, 0)
    for store in stores:
        wait(store)


def run_self_backward(inv, starts, g1, x, q, k, v, att, norms, slots, grads):
    rows = g1.shape[0]
    four = pltpu.VMEM((4, D, D), BF)
    low = pltpu.VMEM((rows, D), BF)
    pad = pltpu.VMEM((rows + QB, D), BF)
    wide = pltpu.VMEM((rows + QB, D), F32)
    sem = pltpu.SemaphoreType.DMA((4, PER))
    return call(
        self_backward,
        (
            jax.ShapeDtypeStruct((rows, D), BF),
            jax.ShapeDtypeStruct((2, D), F32),
            jax.ShapeDtypeStruct(slots.shape, BF),
        ),
        [SM, SM] + [VM] * 7 + [ANY, ANY],
        (VM, VM, ANY),
        [
            four, four, low, low, pad, pad, wide, wide, low, low,
            pltpu.VMEM((rows, D), F32), sem, sem,
        ],
        aliases={10: 2},
    )(inv, starts, g1, x, q, k, v, att, norms, slots, grads)


def from_partner(block, axis):
    half = lax.axis_size(axis) // 2
    count = lax.axis_size(axis)
    return lax.ppermute(block, axis, [(i, (i + half) % count) for i in range(count)])


def adamw_update(weight, moment, second, grad_in, rate, decay_rate):
    new_moment = beta_one * moment + (1.0 - beta_one) * grad_in
    new_second = beta_two * second + (1.0 - beta_two) * grad_in * grad_in
    moment_hat = new_moment / (1.0 - beta_one**STEP)
    second_hat = new_second / (1.0 - beta_two**STEP)
    new_weight = weight - rate * (
        moment_hat / (jnp.sqrt(second_hat) + epsilon) + decay_rate * weight
    )
    return (new_weight, new_moment, new_second)


def caption_plan(lengths, picks, rows, images):
    ends = jnp.cumsum(lengths)
    starts = ends - lengths
    rank = picks * lengths.shape[0] + jnp.arange(lengths.shape[0], dtype=jnp.int32)
    ahead = rank[None, :] < rank[:, None]
    sorted_starts = jnp.sum(jnp.where(ahead, lengths[None, :], 0), axis=1)
    token = jnp.arange(rows, dtype=jnp.int32)
    inside = (token[:, None] >= starts[None, :]) & (token[:, None] < ends[None, :])
    place = token + jnp.sum(jnp.where(inside, (sorted_starts - starts)[None, :], 0), axis=1)
    edges = jnp.arange(images + 1, dtype=jnp.int32)
    bounds = jnp.sum(jnp.where(picks[None, :] < edges[:, None], lengths[None, :], 0), axis=1)
    return place, sorted_starts, bounds


def per_device(
    tokens,
    cotangent,
    caption_lengths,
    image_index,
    image_states,
    master_weights,
    first_moments,
    second_moments,
    owner_list,
    norm_params,
    norm_first,
    norm_second,
):
    rows = tokens.shape[0]
    groups = owner_list.shape[0]
    total_rows = 8 * D + 2 * FF
    group_rows = total_rows // groups
    images = image_states.shape[0]
    axes = ("tower", "dp")
    direct = group_rows == GROUP
    gathered = lax.all_gather(master_weights.astype(BF), axes, axis=0, tiled=True)
    ids = jnp.arange(groups, dtype=jnp.int32)
    inverse = jnp.sum(jnp.where(owner_list[None, :] == ids[:, None], ids[None, :], 0), axis=1)
    if direct:
        slots = gathered.reshape(groups, GROUP, D)
        inv = inverse
    else:
        slots = gathered.reshape(groups, group_rows, D)[inverse].reshape(-1, GROUP, D)
        inv = jnp.arange(total_rows // GROUP, dtype=jnp.int32)

    place, own_starts, own_bounds = caption_plan(caption_lengths[0], image_index[0], rows, images)
    into = (place[None, :] == jnp.arange(rows, dtype=jnp.int32)[:, None]).astype(BF)
    plan = from_partner(jnp.concatenate([own_starts, own_bounds]), "tower")
    starts, bounds = plan[: own_starts.shape[0]], plan[own_starts.shape[0] :]
    sent_tokens = jnp.dot(into, tokens, preferred_element_type=F32).astype(BF)
    sent_cot = jnp.dot(into, cotangent, preferred_element_type=F32).astype(BF)
    x = from_partner(sent_tokens, "tower")
    cot = from_partner(sent_cot, "tower")

    img = image_states.reshape(-1, D)
    normed, _i = normalise(img.astype(F32))
    enc = (normed * norm_params[3] + norm_params[7]).astype(BF)

    q, k, v, att, r1, cq = run_self_forward(inv, starts, x, norm_params, slots)
    ck, cv, cross, r2 = run_cross_forward(images, inv, bounds, enc, cq, r1, slots)
    out, g2, ng3, grads = run_feed_forward(inv, r2, cot, norm_params, slots)
    out_back = from_partner(out, "tower")
    g1, grad_images, ng2, grads = run_cross_backward(
        images, inv, bounds, g2, cross, ck, cv, cq, r1, enc, img, norm_params, slots, grads
    )
    gt, ng1, grads = run_self_backward(
        inv, starts, g1, x, q, k, v, att, norm_params, slots, grads
    )
    gt_back = from_partner(gt, "tower")
    layer_out = lax.dot_general(
        into, out_back, (((0,), (0,)), ((), ())), preferred_element_type=F32
    ).astype(BF)
    grad_tokens = lax.dot_general(
        into, gt_back, (((0,), (0,)), ((), ())), preferred_element_type=F32
    )
    if direct:
        arranged = grads.reshape(total_rows, D)
    else:
        arranged = grads.reshape(groups, group_rows, D)[owner_list].reshape(total_rows, D)
    reduced = lax.psum_scatter(arranged, axes, scatter_dimension=0, tiled=True).astype(F32)
    norm_terms = jnp.stack(
        [ng1[0], ng2[0], ng3[0], ng2[2], ng1[1], ng2[1], ng3[1], ng2[3]]
    )
    norm_grads = lax.psum(norm_terms, axes)
    new_weights, new_first, new_second = adamw_update(
        master_weights, first_moments, second_moments, reduced, learn_rate, weight_decay
    )
    norm_new, norm_first_new, norm_second_new = adamw_update(
        norm_params, norm_first, norm_second, norm_grads, norm_rate, 0.0
    )
    return (
        layer_out,
        grad_tokens,
        grad_images.reshape(image_states.shape),
        new_weights,
        new_first,
        new_second,
        new_weights.astype(BF),
        norm_new,
        norm_first_new,
        norm_second_new,
    )


def solution(mesh):
    split = P(("tower", "dp"), None)
    wide = P(("tower", "dp"), None, None)
    in_specs = (split,) * 4 + (wide,) + (split,) * 3 + (P(),) * 4
    out_specs = (split, split, wide) + (split,) * 4 + (P(),) * 3
    return jax.shard_map(
        per_device, mesh=mesh, in_specs=in_specs, out_specs=out_specs, check_vma=False
    )
```

time: 1240 us -> 609 us (0.49)
  matrix products: 418 us -> 10.7 us
  Pallas kernels: 0 us -> 229 us
  local copies, waits for them, and re-layouts: 219 us -> 4.97 us
  other arithmetic: 157 us -> 15.8 us
  waiting for transfers between devices: 375 us -> 235 us
  blocking collectives: 42 us -> 87 us
    dot_general x44 -> x4, matrix products: 418 us -> 10.7 us  [the longest x1 4.06 us: per_device(): lax.dot_general(into, gt_back, (((0,), (0,)), ((), ())), preferred_elemen...]
    pallas_call x0 -> x5, Pallas kernels: none -> 229 us  [the longest x1 85.3 us: run_cross_backward(): call(functools.partial(cross_backward, images), (jax.ShapeDtypeStruct((ro...]
    gather x14 -> x0, local copies, waits for them, and re-layouts: 118 us -> none  [the longest x1 26.2 us: per_device(): logical_grads.reshape(groups, group_rows, D)[owner_list]]
    reduce_scatter x1, waiting for transfers between devices: 193 us -> 107 us  [per_device(): lax.psum_scatter(arranged, axes, scatter_dimension=0, tiled=True)]
    convert_element_type x5 -> x3, other arithmetic: 71.4 us -> 10.9 us  [the longest x1 4.69 us: per_device(): new_weights.astype(BF)]
    reduce_sum x12 -> x6, other arithmetic: 49.3 us -> 2.8 us  [the longest x1 1.17 us: normalise(): jnp.mean(centred * centred, axis=-1, keepdims=True) + norm_eps]
    psum x1, blocking collectives: 42 us -> 87 us  [per_device(): norm_grads = lax.psum(norm_terms, axes)]
    ppermute x2 -> x5, waiting for transfers between devices: 51.9 us -> 18.6 us  [from_partner(): lax.ppermute(block, axis, [(i, (i + half) % count) for i in range(count)])]
  transfers between devices with their start and end apart: 4 -> 7, of which waited for: 3 -> 3; matrix products, arithmetic and copies ran while one was open for 14% -> 4% of each run, Pallas kernels for 0% -> 11%
where the time goes in v1:
time: 609 us; the launch traced here: 604 us
  waiting for transfers between devices  235 us (39%)
  Pallas kernels  229 us (38%)
  blocking collectives  87 us (14%)
  other arithmetic  15.8 us (3%)
  between operations  14.5 us (2%)
  matrix products  10.7 us (2%)
  starting transfers between devices  7.07 us (1%)
    all_gather x1, waiting for transfers between devices, per_device(): lax.all_gather(master_weights.astype(BF), axes, axis=0, tiled=True)  109 us
    reduce_scatter x1, waiting for transfers between devices, per_device(): lax.psum_scatter(arranged, axes, scatter_dimension=0, tiled=True)  107 us
    psum x1, blocking collectives, per_device(): norm_grads = lax.psum(norm_terms, axes)  87 us
    pallas_call x1, Pallas kernels, run_cross_backward(): call(functools.partial(cross_backward, images), (jax.ShapeDtypeStruct((ro...  85.3 us
    pallas_call x1, Pallas kernels, run_cross_forward(): call(functools.partial(cross_forward, images), (kv, kv, jax.ShapeDtypeStr...  43.2 us
    pallas_call x1, Pallas kernels, run_self_backward(): call(self_backward, (jax.ShapeDtypeStruct((rows, D), BF), jax.ShapeDtypeS...  37.4 us
    pallas_call x1, Pallas kernels, run_feed_forward(): call(feed_forward, (jax.ShapeDtypeStruct((rows, D), BF), jax.ShapeDtypeSt...  37 us
    pallas_call x1, Pallas kernels, run_self_forward(): call(self_forward, (one, one, one, one, jax.ShapeDtypeStruct((rows, D), F...  26.2 us
  transfers between devices with their start and end apart: 7, of which 3 were waited for; matrix products, arithmetic and copies ran while one was open for 4% of the time, Pallas kernels for 11%

profile of v1, /device:TPU:0, one launch (start us, length us, event | category | flops | bytes accessed | tf_op | source)
XLA Modules:
  0.0 604.2 jit_solution(12300851764244928261)
XLA Ops:
  7.2 0.0 copy-start
  7.2 0.0 all-gather.2.cloned.1.call-start
  7.3 2.2 convert_element_type.33
  9.5 0.0 all-gather.2.cloned.1.call-update
  9.5 0.0 reduce-scatter.2.cloned.1.call-start
  9.6 0.1 select_reduce_fusion.3
  9.7 0.2 select_reduce_fusion.2
  9.9 0.6 pad_add_fusion
  10.5 2.9 collective-permute-start
  13.4 0.1 copy.26
  13.6 0.1 reduce.2
  13.7 0.1 select_reduce_fusion
  13.8 0.0 copy-start.12
  13.8 2.2 fusion.6
  16.0 2.2 fusion.7
  18.2 2.0 collective-permute-start.2
  20.2 0.6 convert_reduce_fusion
  20.8 1.2 fusion.1
  21.9 0.6 add_rsqrt_fusion
  22.6 0.7 div.39
  23.2 0.8 rsqrt.12
  24.0 0.8 slice_reduce_fusion.1
  24.9 0.0 copy-start.15
  24.9 4.0 add_convert_fusion.enc
  28.9 0.7 select_reduce_fusion.1.inv
  29.6 1.3 slice.36.bounds
  30.8 18.6 %collective-permute-done.1.x = bf16[768,768]{1,0:T(8,128)(2,1)} collective-permute-done((bf16[768,768]{1,0:T(8,128)(2,1)}, bf16[768,768]{1,0:T(8,128)(2,1)}, u32[]{:S(2)}, u32[]{:S(2)}) %collective-permute-start.1) | collective-permute-done | bytes 1179680 | tf_op jit(solution)/shard_map/ppermute | solution.py:627
  49.4 109.3 %all-gather.2.cloned.1.call-done = bf16[12288,768]{1,0:T(8,128)(2,1)} async-done(((bf16[384,768]{1,0:T(8,128)(2,1)}), bf16[12288,768]{1,0:T(8,128)(2,1)}) %all-gather.2.cloned.1.call-update) | async-done | bytes 18874384 | tf_op jit(solution)/shard_map/all_gather | solution.py:676
  158.7 26.2 %shard_map.195 = (bf16[768,768]{1,0:T(8,128)(2,1)}, bf16[768,768]{1,0:T(8,128)(2,1)}, bf16[768,768]{1,0:T(8,128)(2,1)}, bf16[768,768]{1,0:T(8,128)(2,1)}, f32[768,768]{1,0:T(8,128)}, /*index=5*/bf16[768,768]{1,0:T(8,128)(2,1)}) custom-call(s32[64]{0:T(128)} %select_reduce_fusion.1.inv, s32[24]{0:T(128)} %bitcast.29.starts, ...), custom_call_target="tpu_custom_call" | custom-call | tf_op jit(solution)/shard_map/pallas_call | solution.py:198
  185.0 43.2 %shard_map.196 = (bf16[2304,768]{1,0:T(8,128)(2,1)}, bf16[2304,768]{1,0:T(8,128)(2,1)}, bf16[768,768]{1,0:T(8,128)(2,1)}, f32[768,768]{1,0:T(8,128)}) custom-call(s32[64]{0:T(128)} %select_reduce_fusion.1.inv, s32[5]{0:T(128)} %slice.36.bounds, bf16[2304,768]{1,0:T(8,128)(2,1)} %add_convert_fusion.enc, bf16[768,768]{1,0:T(8,128)(2,1)} %get-tuple-element.31.cq, ...), custom_call_target="tpu_custom_call" | custom-call | tf_op jit(solution)/shard_map/pallas_call | solution.py:271
  228.2 37.0 %shard_map.197 = (bf16[768,768]{1,0:T(8,128)(2,1)}, f32[768,768]{1,0:T(8,128)}, f32[2,768]{1,0:T(2,128)}, bf16[64,192,768]{2,1,0:T(8,128)(2,1)}) custom-call(s32[64]{0:T(128)} %select_reduce_fusion.1.inv, f32[768,768]{1,0:T(8,128)} %get-tuple-element.33.r2, bf16[768,768]{1,0:T(8,128)(2,1)} %collective-permute-done.2.cot, f32[8,768]{1,0:T(8,128)} %norms.7, ...), custom_call_target="tpu_custom_call" | custom-call | tf_op jit(solution)/shard_map/pallas_call | solution.py:376
  265.2 85.3 %shard_map.198 = (f32[768,768]{1,0:T(8,128)}, f32[2304,768]{1,0:T(8,128)}, f32[4,768]{1,0:T(4,128)}, bf16[64,192,768]{2,1,0:T(8,128)(2,1)}) custom-call(s32[64]{0:T(128)} %select_reduce_fusion.1.inv, s32[5]{0:T(128)} %slice.36.bounds, f32[768,768]{1,0:T(8,128)} %get-tuple-element.35.g2, ...), custom_call_target="tpu_custom_call", output_to_operand_aliasing={{3}: (12, {})} | custom-call | tf_op jit(solution)/shard_map/pallas_call | solution.py:505
  350.5 37.4 %shard_map.199 = (bf16[768,768]{1,0:T(8,128)(2,1)}, f32[2,768]{1,0:T(2,128)}, bf16[64,192,768]{2,1,0:T(8,128)(2,1)}) custom-call(s32[64]{0:T(128)} %select_reduce_fusion.1.inv, s32[24]{0:T(128)} %bitcast.29.starts, f32[768,768]{1,0:T(8,128)} %get-tuple-element.40.g1, bf16[768,768]{1,0:T(8,128)(2,1)} %collective-permute-done.1.x, ...), custom_call_target="tpu_custom_call", output_to_operand_aliasing={{2}: (10, {})} | custom-call | tf_op jit(solution)/shard_map/pallas_call | solution.py:607
  387.9 0.0 copy-start.9
  387.9 0.0 copy-start.10
  387.9 0.0 copy-start.6
  388.0 0.0 copy-start.7
  388.0 0.0 reduce-scatter.2.cloned.1.call-update
  388.0 1.2 copy-done.13
  389.2 1.4 collective-permute-start.3
  390.6 0.6 collective-permute-start.4
  391.3 0.1 stack.3
  391.3 87.0 %psum.7 = f32[8,768]{1,0:T(8,128)S(1)} all-reduce(f32[8,768]{1,0:T(8,128)S(1)} %stack.3), channel_id=1, replica_groups=mesh['tower'=2,'dp'=16] {'tower','dp'}, use_global_device_ids=true, to_apply=%region_8.9 | all-reduce | flops 6144 | bytes 49152 | tf_op jit(solution)/shard_map/psum | solution.py:724
  478.4 0.6 multiply_subtract_fusion.1
  479.0 2.3 fusion.8
  481.3 4.1 fusion.2
  485.3 107.0 %reduce-scatter.2.cloned.1.call-done = bf16[384,768]{1,0:T(8,128)(2,1)} async-done(((bf16[12288,768]{1,0:T(8,128)(2,1)}), bf16[384,768]{1,0:T(8,128)(2,1)}) %reduce-scatter.2.cloned.1.call-update) | async-done | bytes 589840 | tf_op jit(solution)/shard_map/reduce_scatter | solution.py:720
  592.4 4.7 fusion.20
  (38 shorter events, 0.2 us)
Async XLA Ops:
  7.2 6.6 %copy-start = (bf16[768,768]{1,0:T(8,128)(2,1)S(1)}, bf16[768,768]{1,0:T(8,128)(2,1)}, u32[]{:S(2)}) copy-start(bf16[768,768]{1,0:T(8,128)(2,1)} %param.12) | copy-start | bytes 3538948
  7.2 2.4 copy-start.11
  7.2 2.4 copy-start.14
  7.2 151.5 %all-gather.2.cloned.1.call-start = ((), (), s32[]{:S(2)}) async-start(), calls=%async_computation.1 | async-start | bytes 19464192 | tf_op jit(solution)/shard_map/all_gather | solution.py:676
  9.5 582.9 %reduce-scatter.2.cloned.1.call-start = ((), (), s32[]{:S(2)}) async-start(), calls=%async_computation.2 | async-start | bytes 19464192 | tf_op jit(solution)/shard_map/reduce_scatter | solution.py:720
  10.5 19.1 %collective-permute-start = (s32[29]{0:T(128)}, s32[29]{0:T(128)}, u32[]{:S(2)}, u32[]{:S(2)}) collective-permute-start(s32[29]{0:T(128)} %pad_add_fusion), channel_id=1, source_target_pairs={{0,16},{16,0},{1,17},{17,1},{2,18},{18,2},{3,19},{19,3},{4,20},{20... | collective-permute-start | bytes 356 | tf_op jit(solution)/shard_map/ppermute | solution.py:627
  13.8 2.2 copy-start.12
  16.0 33.4 %collective-permute-start.1 = (bf16[768,768]{1,0:T(8,128)(2,1)}, bf16[768,768]{1,0:T(8,128)(2,1)}, u32[]{:S(2)}, u32[]{:S(2)}) collective-permute-start(bf16[768,768]{1,0:T(8,128)(2,1)} %fusion.6), channel_id=1, source_target_pairs={{0,16},{16,0},{1,17},{17,1},{2,18},{18,2},{3,19},{19,3},{4,20},{20... | collective-permute-start | bytes 3538952 | tf_op jit(solution)/shard_map/ppermute | solution.py:627
  16.0 4.2 copy-start.2
  18.2 210.0 %collective-permute-start.2 = (bf16[768,768]{1,0:T(8,128)(2,1)}, bf16[768,768]{1,0:T(8,128)(2,1)}, u32[]{:S(2)}, u32[]{:S(2)}) collective-permute-start(bf16[768,768]{1,0:T(8,128)(2,1)} %fusion.7), channel_id=1, source_target_pairs={{0,16},{16,0},{1,17},{17,1},{2,18},{18,2},{3,19},{19,3},{4,20},{20... | collective-permute-start | bytes 3538952 | tf_op jit(solution)/shard_map/ppermute | solution.py:627
  24.9 4.0 copy-start.15
  387.9 1.3 copy-start.13
  387.9 3.3 copy-start.9
  387.9 3.3 copy-start.10
  387.9 3.3 copy-start.8
  387.9 90.4 %copy-start.5 = (f32[8,768]{1,0:T(8,128)S(1)}, f32[8,768]{1,0:T(8,128)}, u32[]{:S(2)}) copy-start(f32[8,768]{1,0:T(8,128)} %norms.7) | copy-start | bytes 73732
  387.9 90.4 %copy-start.6 = (f32[8,768]{1,0:T(8,128)S(1)}, f32[8,768]{1,0:T(8,128)}, u32[]{:S(2)}) copy-start(f32[8,768]{1,0:T(8,128)} %param.22) | copy-start | bytes 73732
  388.0 90.4 %copy-start.7 = (f32[8,768]{1,0:T(8,128)S(1)}, f32[8,768]{1,0:T(8,128)}, u32[]{:S(2)}) copy-start(f32[8,768]{1,0:T(8,128)} %param.23) | copy-start | bytes 73732
  389.2 89.9 %collective-permute-start.3 = (bf16[768,768]{1,0:T(8,128)(2,1)S(1)}, bf16[768,768]{1,0:T(8,128)(2,1)S(1)}, u32[]{:S(2)}, u32[]{:S(2)}) collective-permute-start(bf16[768,768]{1,0:T(8,128)(2,1)S(1)} %copy-done.13), channel_id=1, source_target_pairs={{0,16},{16,0},{1,17},{17,1},{2,18},{18,2},{3,19},{19,3},{4,20},{20... | collective-permute-start | bytes 3538952 | tf_op jit(solution)/shard_map/ppermute | solution.py:627
  390.6 90.7 %collective-permute-start.4 = (bf16[768,768]{1,0:T(8,128)(2,1)}, bf16[768,768]{1,0:T(8,128)(2,1)}, u32[]{:S(2)}, u32[]{:S(2)}) collective-permute-start(bf16[768,768]{1,0:T(8,128)(2,1)} %get-tuple-element.46), channel_id=1, source_target_pairs={{0,16},{16,0},{1,17},{17,1},{2,18},{18,2},{3,19},{19,3},{4,20},{20... | collective-permute-start | bytes 3538952 | tf_op jit(solution)/shard_map/ppermute | solution.py:627
  481.3 111.1 %copy-start.3 = (f32[384,768]{1,0:T(8,128)S(1)}, f32[384,768]{1,0:T(8,128)}, u32[]{:S(2)}) copy-start(f32[384,768]{1,0:T(8,128)} %param.17) | copy-start | bytes 3538948
  481.3 111.1 %copy-start.4 = (f32[384,768]{1,0:T(8,128)S(1)}, f32[384,768]{1,0:T(8,128)}, u32[]{:S(2)}) copy-start(f32[384,768]{1,0:T(8,128)} %param.18) | copy-start | bytes 3538948
  592.4 4.7 copy-start.1
Sparse Core Ops, SparseCore 0:
  11.5 147.1 all-gather.1
  388.1 204.2 reduce-scatter.1

commit v2 on v1

--- a/solution.py
+++ b/solution.py
@@ -16,6 +16,7 @@
 LANES = 2 * HDIM
 QB = 128
 GROUP = 192
+BOUND_LANE = 64
 PER = D // GROUP
 SCALE = HDIM ** (-0.5)
 
@@ -112,11 +113,11 @@
         copy.wait()
 
 
-def causal_mask(starts, b):
+def causal_mask(meta, captions, b):
     query = lax.broadcasted_iota(jnp.int32, (1, QB), 1) + b * QB
     first = jnp.zeros((1, QB), jnp.int32)
-    for c in range(starts.shape[0]):
-        first = jnp.maximum(first, jnp.where(query >= starts[c], starts[c], 0))
+    for c in range(captions):
+        first = jnp.maximum(first, jnp.where(query >= meta[0, c], meta[0, c], 0))
     key = lax.broadcasted_iota(jnp.int32, (2 * QB, QB), 0) + (b - 1) * QB
     allowed = (key >= first) & (key <= query)
     return jnp.concatenate([allowed, allowed], axis=1)
@@ -129,7 +130,7 @@
 
 
 def self_forward(
-    inv, starts, x, norms, slots, q_o, k_o, v_o, att_o, r1_o, cq_o, wbuf, low, kpad, vpad, wsem
+    captions, inv, meta, x, norms, slots, q_o, k_o, v_o, att_o, r1_o, cq_o, wbuf, low, kpad, vpad, wsem
 ):
     rows = x.shape[0]
     loads = [weight_copies(slots, inv, wbuf, wsem, m, m) for m in range(5)]
@@ -155,7 +156,7 @@
     v_o[...] = vpad[pl.ds(QB, rows), :]
 
     def attend(b, _):
-        allowed = causal_mask(starts, b)
+        allowed = causal_mask(meta, captions, b)
         for p in range(PAIRS):
             q2 = two_heads(q_o[blk(b), lanes(p)], masks)
             keys = kpad[pl.ds(pl.multiple_of(b * QB, QB), 2 * QB), lanes(p)]
@@ -192,11 +193,11 @@
     )
 
 
-def run_self_forward(inv, starts, x, norms, slots):
+def run_self_forward(captions, inv, meta, x, norms, slots):
     rows = x.shape[0]
     one = jax.ShapeDtypeStruct((rows, D), BF)
     return call(
-        self_forward,
+        functools.partial(self_forward, captions),
         (one, one, one, one, jax.ShapeDtypeStruct((rows, D), F32), one),
         [SM, SM, VM, VM, ANY],
         (VM,) * 6,
@@ -207,18 +208,18 @@
             pltpu.VMEM((rows + QB, D), BF),
             pltpu.SemaphoreType.DMA((5, PER)),
         ],
-    )(inv, starts, x, norms, slots)
-
-
-def image_blocks(bounds, i):
-    low, high = bounds[i], bounds[i + 1]
+    )(inv, meta, x, norms, slots)
+
+
+def image_blocks(meta, i):
+    low, high = meta[0, BOUND_LANE + i], meta[0, BOUND_LANE + i + 1]
     first = low // QB
     last = jnp.where(high > low, (high + QB - 1) // QB, first)
     return low, high, first, last
 
 
 def cross_forward(
-    images, inv, bounds, enc, cq, r1, slots, k_o, v_o, cross_o, r2_o, wbuf, acc, wsem
+    images, inv, meta, enc, cq, r1, slots, k_o, v_o, cross_o, r2_o, wbuf, acc, wsem
 ):
     patches = enc.shape[0] // images
     loads = [weight_copies(slots, inv, wbuf, wsem, m, i) for i, m in enumerate((C_K, C_V, C_O))]
@@ -236,7 +237,7 @@
         lax.fori_loop(0, enc.shape[0] // D, project, 0)
 
     def image(i, _):
-        low, high, first, last = image_blocks(bounds, i)
+        low, high, first, last = image_blocks(meta, i)
 
         def attend(b, _):
             token = lax.broadcasted_iota(jnp.int32, (1, QB), 1) + b * QB
@@ -265,7 +266,7 @@
     return pl.ds(pl.multiple_of(i * size, 64), size)
 
 
-def run_cross_forward(images, inv, bounds, enc, cq, r1, slots):
+def run_cross_forward(images, inv, meta, enc, cq, r1, slots):
     rows = cq.shape[0]
     kv = jax.ShapeDtypeStruct(enc.shape, BF)
     return call(
@@ -278,7 +279,7 @@
             pltpu.VMEM((rows, D), F32),
             pltpu.SemaphoreType.DMA((3, PER)),
         ],
-    )(inv, bounds, enc, cq, r1, slots)
+    )(inv, meta, enc, cq, r1, slots)
 
 
 GELU_A = 0.7978845608028654
@@ -388,7 +389,7 @@
 
 
 def cross_backward(
-    images, inv, bounds, g2, cross, k, v, cq, r1, enc, img, norms, slots, grads_in,
+    images, inv, meta, g2, cross, k, v, cq, r1, enc, img, norms, slots, grads_in,
     g1_o, gi_o, ng_o, grads,
     wbuf, gbuf, gca, dq, acck, accv, dk, dv, big, wsem, gsem,
 ):
@@ -410,7 +411,7 @@
     dq[...] = jnp.zeros_like(dq)
 
     def image(i, _):
-        first_row, end_row, first, last = image_blocks(bounds, i)
+        first_row, end_row, first, last = image_blocks(meta, i)
         acck[...] = jnp.zeros_like(acck)
         accv[...] = jnp.zeros_like(accv)
 
@@ -494,7 +495,7 @@
         wait(store)
 
 
-def run_cross_backward(images, inv, bounds, g2, cross, k, v, cq, r1, enc, img, norms, slots, grads):
+def run_cross_backward(images, inv, meta, g2, cross, k, v, cq, r1, enc, img, norms, slots, grads):
     rows = g2.shape[0]
     patches = enc.shape[0] // images
     four = pltpu.VMEM((4, D, D), BF)
@@ -514,11 +515,11 @@
         (VM, VM, VM, ANY),
         [four, four, low, low, part, part, wide, wide, pltpu.VMEM((D, D), F32), sem, sem],
         aliases={12: 3},
-    )(inv, bounds, g2, cross, k, v, cq, r1, enc, img, norms, slots, grads)
+    )(inv, meta, g2, cross, k, v, cq, r1, enc, img, norms, slots, grads)
 
 
 def self_backward(
-    inv, starts, g1, x, q, k, v, att, norms, slots, grads_in,
+    captions, inv, meta, g1, x, q, k, v, att, norms, slots, grads_in,
     gt_o, ng_o, grads,
     wbuf, gbuf, ga, dq, kpad, vpad, acck, accv, dk, dv, big, wsem, gsem,
 ):
@@ -544,7 +545,7 @@
     accv[...] = jnp.zeros_like(accv)
 
     def attend(b, _):
-        allowed = causal_mask(starts, b)
+        allowed = causal_mask(meta, captions, b)
         span = pl.ds(pl.multiple_of(b * QB, QB), 2 * QB)
         for p in range(PAIRS):
             q2 = two_heads(q[blk(b), lanes(p)], masks)
@@ -597,7 +598,7 @@
         wait(store)
 
 
-def run_self_backward(inv, starts, g1, x, q, k, v, att, norms, slots, grads):
+def run_self_backward(captions, inv, meta, g1, x, q, k, v, att, norms, slots, grads):
     rows = g1.shape[0]
     four = pltpu.VMEM((4, D, D), BF)
     low = pltpu.VMEM((rows, D), BF)
@@ -605,7 +606,7 @@
     wide = pltpu.VMEM((rows + QB, D), F32)
     sem = pltpu.SemaphoreType.DMA((4, PER))
     return call(
-        self_backward,
+        functools.partial(self_backward, captions),
         (
             jax.ShapeDtypeStruct((rows, D), BF),
             jax.ShapeDtypeStruct((2, D), F32),
@@ -618,7 +619,531 @@
             pltpu.VMEM((rows, D), F32), sem, sem,
         ],
         aliases={10: 2},
-    )(inv, starts, g1, x, q, k, v, att, norms, slots, grads)
+    )(inv, meta, g1, x, q, k, v, att, norms, slots, grads)
+
+
+MESH = pl.DeviceIdType.MESH
+PART_ROWS = (256, 128)
+PART_OFF = (0, 256)
+X_, Y_, UP_, DN_ = 0, 1, 2, 3
+OPPOSITE = (X_, Y_, DN_, UP_)
+ARRIVALS = (
+    (1, 1, 0, 0), (0, 0, 0, 1), (0, 0, 1, 0), (1, 0, 1, 0), (1, 0, 0, 1), (0, 1, 0, 0),
+    (1, 1, 1, 0), (1, 1, 0, 1), (0, 0, 2, 0), (1, 0, 1, 1), (0, 0, 1, 1), (1, 0, 2, 0),
+    (1, 1, 1, 1), (0, 1, 0, 1), (1, 1, 2, 0), (0, 0, 2, 1), (0, 1, 1, 0), (0, 0, 3, 0),
+    (1, 0, 2, 1), (1, 0, 3, 0), (1, 1, 2, 1), (0, 1, 2, 0), (0, 1, 1, 1), (0, 1, 3, 0),
+    (0, 0, 3, 1), (1, 1, 3, 0), (1, 0, 3, 1), (0, 1, 2, 1), (1, 1, 3, 1), (0, 1, 3, 1),
+)
+OWN_SENDS = (
+    (1, X_), (0, Y_), (0, UP_), (0, DN_), (1, UP_), (1, DN_), (1, Y_), (0, X_),
+)
+Z_CHIPS = 4
+
+
+def signed_arrivals():
+    for part, dt, dz, dy in ARRIVALS:
+        for step in (-dz, dz) if dz else (0,):
+            yield part, dt, step, dy
+
+
+def routes(part, dt, dz, dy):
+    along = [UP_] * (dz <= 0) + [DN_] * (dz >= 0)
+    if part == 0:
+        return [] if dy else [Y_] if dt else along + [X_, Y_]
+    return along if dz or dy else along + [Y_] if dt else [X_, Y_] + along
+
+
+def source(part, dt, dz, dy):
+    last = UP_ if dz > 0 else DN_
+    if part == 0:
+        return Y_ if dy else X_ if dt else last
+    return last if dz else Y_ if dy else X_
+
+
+class Place:
+    def __init__(self):
+        self.t = lax.axis_index("tower")
+        d = lax.axis_index("dp")
+        self.z, self.y, self.c = d // 4, (d // 2) % 2, d % 2
+
+    def device(self, t, z, y, c):
+        return (t, z * 4 + y * 2 + c)
+
+    def neighbour(self, kind):
+        t, z, y, c = self.t, self.z, self.y, self.c
+        return (
+            self.device(1 - t, z, y, c),
+            self.device(t, z, 1 - y, c),
+            self.device(t, jnp.minimum(z + 1, Z_CHIPS - 1), y, c),
+            self.device(t, jnp.maximum(z - 1, 0), y, c),
+        )[kind]
+
+    def line(self):
+        return [
+            self.device(self.t, lax.rem(self.z + k, Z_CHIPS), self.y, self.c)
+            for k in range(1, Z_CHIPS)
+        ]
+
+    def sibling(self):
+        return self.device(self.t, self.z, self.y, 1 - self.c)
+
+    def has(self, kind):
+        return {UP_: self.z < Z_CHIPS - 1, DN_: self.z > 0}.get(kind)
+
+    def chip(self, dt=0, dz=0, dy=0):
+        t = 1 - self.t if dt else self.t
+        y = 1 - self.y if dy else self.y
+        return t * 8 + (self.z + dz) * 2 + y
+
+    def exists(self, dz):
+        return None if dz == 0 else self.z >= -dz if dz < 0 else self.z < Z_CHIPS - dz
+
+
+def rows_of(chip, core, part):
+    return pl.ds(
+        pl.multiple_of((chip * 2 + core) * sum(PART_ROWS) + PART_OFF[part], 128), PART_ROWS[part]
+    )
+
+
+def both(first, second):
+    return second if first is None else first if second is None else first & second
+
+
+def when(condition, body):
+    if condition is None:
+        body()
+    else:
+        pl.when(condition)(body)
+
+
+def greet(place, whole_line):
+    barrier = pltpu.get_barrier_semaphore()
+    targets = [place.neighbour(X_), place.neighbour(Y_), place.sibling()]
+    if whole_line:
+        targets += place.line()
+    for target in targets:
+        pl.semaphore_signal(barrier, inc=1, device_id=target, device_id_type=MESH)
+    if whole_line:
+        pl.semaphore_wait(barrier, len(targets))
+        return
+    for kind in (UP_, DN_):
+
+        @pl.when(place.has(kind))
+        def _(kind=kind):
+            pl.semaphore_signal(
+                barrier, inc=1, device_id=place.neighbour(kind), device_id_type=MESH
+            )
+
+    inner = (place.z > 0) & (place.z < Z_CHIPS - 1)
+    pl.semaphore_wait(barrier, jnp.where(inner, len(targets) + 2, len(targets) + 1))
+
+
+def plan_captions(lengths, picks, start_s, sorted_s, bound_s, images):
+    captions = lengths.shape[1]
+
+    def begin(c, run):
+        start_s[c] = run
+        return run + lengths[0, c]
+
+    lax.fori_loop(0, captions, begin, jnp.int32(0))
+
+    def image(i, run):
+        bound_s[i] = run
+
+        def caption(c, run):
+            hit = picks[0, c] == i
+            sorted_s[c] = jnp.where(hit, run, sorted_s[c])
+            return run + jnp.where(hit, lengths[0, c], 0)
+
+        return lax.fori_loop(0, captions, caption, run)
+
+    def clear(c, run):
+        sorted_s[c] = 0
+        return run
+
+    lax.fori_loop(0, captions, clear, 0)
+    bound_s[images] = lax.fori_loop(0, images, image, jnp.int32(0))
+
+
+def gather_kernel(
+    images, lengths, picks, tokens, cot, img, master, norms,
+    slots, x_o, meta_o, cot_o, enc_o, place_o,
+    own, xs, metas, start_s, sorted_s, bound_s,
+    ssem, rsem, sibsem, sibrecv, xsem, lsem,
+):
+    place = Place()
+    rows = tokens.shape[0]
+    captions = lengths.shape[1]
+    own[...] = master[...].astype(BF)
+    greet(place, False)
+    sends = []
+
+    def push(condition, part, chip, kind, mine=False):
+        target = place.sibling() if kind == 4 else place.neighbour(kind)
+        if kind < 4:
+            condition = both(condition, place.has(kind))
+        rows_p = rows_of(chip, place.c, part)
+        src = own.at[pl.ds(PART_OFF[part], PART_ROWS[part])] if mine else slots.at[rows_p]
+        sem = sibrecv if kind == 4 else rsem
+        out = sibsem.at[part, chip] if kind == 4 else ssem.at[kind, part, chip]
+        copy = pltpu.make_async_remote_copy(
+            src_ref=src, dst_ref=slots.at[rows_p], send_sem=out, recv_sem=sem.at[part, chip],
+            device_id=target, device_id_type=MESH,
+        )
+        when(condition, copy.start)
+        sends.append((condition, copy))
+
+    me = place.chip()
+    for part, kind in OWN_SENDS + ((0, 4), (1, 4)):
+        push(None, part, me, kind, mine=True)
+    keep = pltpu.make_async_copy(
+        own, slots.at[pl.ds(pl.multiple_of((me * 2 + place.c) * own.shape[0], 128), own.shape[0])], lsem
+    )
+    keep.start()
+
+    plan_captions(lengths, picks, start_s, sorted_s, bound_s, images)
+    token = lax.broadcasted_iota(jnp.int32, (1, rows), 1)
+
+    def locate(c, where_to):
+        inside = (token >= start_s[c]) & (token < start_s[c] + lengths[0, c])
+        return jnp.where(inside, token + (sorted_s[c] - start_s[c]), where_to)
+
+    where_to = lax.fori_loop(0, captions, locate, token)
+    place_o[...] = jnp.broadcast_to(where_to, place_o.shape)
+    lane = lax.broadcasted_iota(jnp.int32, metas.shape, 1)
+
+    def note(c, row):
+        return jnp.where(lane == c, sorted_s[c], row)
+
+    row = lax.fori_loop(0, captions, note, jnp.zeros(metas.shape, jnp.int32))
+    for i in range(images + 1):
+        row = jnp.where(lane == BOUND_LANE + i, bound_s[i], row)
+    metas[...] = row
+
+    def sort(out, array):
+        def body(b, _):
+            target = lax.broadcasted_iota(jnp.int32, (QB, rows), 0) + b * QB
+            onehot = (target == place_o[0:1, :]).astype(F32).astype(BF)
+            out[blk(b), :] = nn(onehot, array[...]).astype(BF)
+            return 0
+
+        lax.fori_loop(0, rows // QB, body, 0)
+
+    sort(xs, tokens)
+    swaps = []
+    for i, (src, dst) in enumerate(((metas, meta_o), (xs, x_o))):
+        swaps.append(
+            pltpu.make_async_remote_copy(
+                src_ref=src, dst_ref=dst, send_sem=xsem.at[0, i], recv_sem=xsem.at[1, i],
+                device_id=place.neighbour(X_), device_id_type=MESH,
+            )
+        )
+        swaps[-1].start()
+
+    def encode(i):
+        def body(j, _):
+            at = pl.ds(pl.multiple_of(i * IMG_ROWS + j * 64, 64), 64)
+            normed, _i = normalise(img[at, :].astype(F32))
+            enc_o[at, :] = (normed * norms[3:4, :] + norms[7:8, :]).astype(BF)
+            return 0
+
+        lax.fori_loop(0, IMG_ROWS // 64, body, 0)
+
+    steps = img.shape[0] // IMG_ROWS
+    done = 0
+    for number, (part, dt, dz, dy) in enumerate(signed_arrivals()):
+        there = place.exists(dz)
+        chip = place.chip(dt, dz, dy)
+
+        def arrived(part=part, chip=chip):
+            rows_p = rows_of(chip, place.c, part)
+            pltpu.make_async_remote_copy(
+                src_ref=slots.at[rows_p], dst_ref=slots.at[rows_p], send_sem=ssem.at[0, part, chip],
+                recv_sem=rsem.at[part, chip], device_id=place.neighbour(X_), device_id_type=MESH,
+            ).wait_recv()
+
+        when(there, arrived)
+        for kind in routes(part, dt, dz, dy) + [4]:
+            push(there, part, chip, kind)
+        if number == 4:
+            sort(cot_o, cot)
+        if number >= 6 and done < steps:
+            encode(done)
+            done += 1
+    for i in range(done, steps):
+        encode(i)
+
+    def from_sibling(chip, _):
+        for part in range(2):
+            rows_p = rows_of(chip, 1 - place.c, part)
+            pltpu.make_async_remote_copy(
+                src_ref=slots.at[rows_p], dst_ref=slots.at[rows_p], send_sem=sibsem.at[part, chip],
+                recv_sem=sibrecv.at[part, chip], device_id=place.sibling(), device_id_type=MESH,
+            ).wait_recv()
+        return 0
+
+    lax.fori_loop(0, 4 * Z_CHIPS, from_sibling, 0)
+    for condition, copy in sends:
+        when(condition, copy.wait_send)
+    for swap in swaps:
+        swap.wait()
+    keep.wait()
+
+
+IMG_ROWS = 192
+
+
+def run_gather(images, lengths, picks, tokens, cot, img, master, norms, total_rows):
+    rows = tokens.shape[0]
+    dma = pltpu.SemaphoreType.DMA
+    low = jax.ShapeDtypeStruct((rows, D), BF)
+    return pl.pallas_call(
+        functools.partial(gather_kernel, images),
+        out_shape=(
+            jax.ShapeDtypeStruct((total_rows, D), BF),
+            low,
+            jax.ShapeDtypeStruct((8, 128), jnp.int32),
+            low,
+            jax.ShapeDtypeStruct(img.shape, BF),
+            jax.ShapeDtypeStruct((8, rows), jnp.int32),
+        ),
+        in_specs=[SM, SM, VM, VM, VM, VM, VM],
+        out_specs=(ANY, ANY, ANY, VM, VM, VM),
+        scratch_shapes=[
+            pltpu.VMEM(master.shape, BF),
+            pltpu.VMEM((rows, D), BF),
+            pltpu.VMEM((8, 128), jnp.int32),
+            pltpu.SMEM((lengths.shape[1],), jnp.int32),
+            pltpu.SMEM((lengths.shape[1],), jnp.int32),
+            pltpu.SMEM((images + 1,), jnp.int32),
+            dma((4, 2, 16)),
+            dma((2, 16)),
+            dma((2, 16)),
+            dma((2, 16)),
+            dma((2, 2)),
+            dma,
+        ],
+        compiler_params=pltpu.CompilerParams(
+            vmem_limit_bytes=VLIM, has_side_effects=True, collective_id=0
+        ),
+    )(lengths, picks, tokens, cot, img, master, norms)
+
+
+def sum_kernel(
+    grads, norm_terms, place_row, gt, out_back,
+    red_o, norm_o, gt_o, lay_o,
+    acc, sib, ya, xa, ba, aa, zb_b, zb_a, yb, xb, gtr, nbuf, nrecv,
+    lsem, sibsem, sibrecv, ssem, rsem, gsem, nsend, nrs,
+):
+    place = Place()
+    rows = gt.shape[0]
+    greet(place, True)
+    order = list(signed_arrivals())[::-1] + [(0, 0, 0, 0), (1, 0, 0, 0)]
+    sends = []
+
+    def local(part, chip):
+        off = pl.ds(PART_OFF[part], PART_ROWS[part])
+        return pltpu.make_async_copy(
+            grads.at[rows_of(chip, place.c, part)], acc.at[chip, off], lsem.at[part, chip]
+        )
+
+    def across(part, chip):
+        off = pl.ds(PART_OFF[part], PART_ROWS[part])
+        return pltpu.make_async_remote_copy(
+            src_ref=grads.at[rows_of(chip, 1 - place.c, part)], dst_ref=sib.at[chip, off],
+            send_sem=sibsem.at[part, chip], recv_sem=sibrecv.at[part, chip],
+            device_id=place.sibling(), device_id_type=MESH,
+        )
+
+    for part, dt, dz, dy in order:
+        chip = place.chip(dt, dz, dy)
+
+        def begin(part=part, chip=chip):
+            across(part, chip).start()
+            local(part, chip).start()
+
+        when(place.exists(dz), begin)
+    back = pltpu.make_async_remote_copy(
+        src_ref=gt, dst_ref=gtr, send_sem=gsem.at[0], recv_sem=gsem.at[1],
+        device_id=place.neighbour(X_), device_id_type=MESH,
+    )
+    back.start()
+
+    def landing(part, kind, chip):
+        t, z = chip // 8, (chip // 2) % Z_CHIPS
+        if part == 0:
+            ref, index = {X_: (xa, z), Y_: (ya, t * Z_CHIPS + z), UP_: (ba, z), DN_: (aa, z)}[kind]
+        else:
+            ref, index = {X_: (xb, 0), Y_: (yb, t), UP_: (zb_b, chip), DN_: (zb_a, chip)}[kind]
+        return ref.at[index]
+
+    def flow(part, kind, chip):
+        off = pl.ds(PART_OFF[part], PART_ROWS[part])
+        return pltpu.make_async_remote_copy(
+            src_ref=acc.at[chip, off], dst_ref=landing(part, kind, chip),
+            send_sem=ssem.at[part, chip], recv_sem=rsem.at[kind, part, chip],
+            device_id=place.neighbour(kind), device_id_type=MESH,
+        )
+
+    def add(part, chip, other, final):
+        def body(i, _):
+            at = pl.ds(pl.multiple_of(PART_OFF[part] + i * 64, 64), 64)
+            value = acc[chip, at, :].astype(F32)
+            for ref in other:
+                value = value + ref(part, pl.ds(pl.multiple_of(i * 64, 64), 64), at).astype(F32)
+            if final:
+                red_o[at, :] = value
+            else:
+                acc[chip, at, :] = value.astype(BF)
+            return 0
+
+        lax.fori_loop(0, PART_ROWS[part] // 64, body, 0)
+
+    def norm_round(i, target):
+        return pltpu.make_async_remote_copy(
+            src_ref=nbuf.at[i], dst_ref=nrecv.at[i], send_sem=nsend.at[i], recv_sem=nrs.at[i],
+            device_id=target, device_id_type=MESH,
+        )
+
+    def norm_line(k, target):
+        return pltpu.make_async_remote_copy(
+            src_ref=nbuf.at[3], dst_ref=nrecv.at[3 + place.z], send_sem=nsend.at[3 + k],
+            recv_sem=nrs.at[3 + place.z], device_id=target, device_id_type=MESH,
+        )
+
+    def norm_from(z):
+        return pltpu.make_async_remote_copy(
+            src_ref=nbuf.at[3], dst_ref=nrecv.at[3 + z], send_sem=nsend.at[3], recv_sem=nrs.at[3 + z],
+            device_id=place.neighbour(X_), device_id_type=MESH,
+        )
+
+    line = [norm_line(k, target) for k, target in enumerate(place.line())]
+    rounds = [place.sibling(), place.neighbour(X_), place.neighbour(Y_)]
+    nbuf[0] = norm_terms[...]
+    norm_round(0, rounds[0]).start()
+
+    def unsort(out, array):
+        def body(b, _):
+            target = lax.broadcasted_iota(jnp.int32, (rows, QB), 0)
+            onehot = (target == place_row[0:1, blk(b)]).astype(F32).astype(BF)
+            out[blk(b), :] = tn(onehot, array[...]).astype(out.dtype)
+            return 0
+
+        lax.fori_loop(0, rows // QB, body, 0)
+
+    for number, (part, dt, dz, dy) in enumerate(order):
+        chip = place.chip(dt, dz, dy)
+        there = place.exists(dz)
+        final = (dt, dz, dy) == (0, 0, 0)
+        kinds = routes(part, dt, dz, dy)
+
+        def step(part=part, chip=chip, kinds=kinds, final=final, dt=dt, dz=dz, dy=dy):
+            local(part, chip).wait()
+            across(part, chip).wait_recv()
+            refs = [lambda p, i, at: sib[chip, at, :]]
+            fixed = [kind for kind in kinds if kind in (X_, Y_)]
+            edge = [kind for kind in kinds if kind in (UP_, DN_)]
+            for kind in fixed:
+                flow(part, OPPOSITE[kind], chip).wait_recv()
+                refs.append(
+                    lambda p, i, at, kind=kind: landing(part, OPPOSITE[kind], chip)[i, :]
+                )
+            for kind in edge:
+
+                def one(kind=kind):
+                    flow(part, OPPOSITE[kind], chip).wait_recv()
+                    add(part, chip, [lambda p, i, at: landing(part, OPPOSITE[kind], chip)[i, :]], False)
+
+                pl.when(place.has(kind))(one)
+            add(part, chip, refs, final)
+            if not final:
+                flow(part, source(part, dt, dz, dy), chip).start()
+
+        when(there, step)
+        if not final:
+            sends.append((there, part, chip, source(part, dt, dz, dy)))
+        if number in (12, 20, 28):
+            i = (12, 20, 28).index(number)
+            norm_round(i, rounds[i]).wait()
+            nbuf[i + 1] = nbuf[i] + nrecv[i]
+            if i < 2:
+                norm_round(i + 1, rounds[i + 1]).start()
+            else:
+                for copy in line:
+                    copy.start()
+        if number == 16:
+            unsort(lay_o, out_back)
+        if number == 40:
+            back.wait()
+            unsort(gt_o, gtr)
+
+    for z in range(Z_CHIPS):
+
+        @pl.when(place.z != z)
+        def _(z=z):
+            norm_from(z).wait_recv()
+
+        @pl.when(place.z == z)
+        def _(z=z):
+            nrecv[3 + z] = nbuf[3]
+
+    norm_o[...] = (nrecv[3] + nrecv[4]) + (nrecv[5] + nrecv[6])
+    for copy in line:
+        copy.wait_send()
+    for there, part, chip, kind in sends:
+        when(there, flow(part, kind, chip).wait_send)
+
+    def sent(chip, _):
+        for part in range(2):
+            across(part, chip).wait_send()
+        return 0
+
+    lax.fori_loop(0, 4 * Z_CHIPS, sent, 0)
+
+
+def run_sum(grads, norm_terms, place_row, gt, out_back):
+    rows = gt.shape[0]
+    dma = pltpu.SemaphoreType.DMA
+    a, b = PART_ROWS
+    shard = a + b
+    line = 4 * Z_CHIPS
+    return pl.pallas_call(
+        sum_kernel,
+        out_shape=(
+            jax.ShapeDtypeStruct((shard, D), F32),
+            jax.ShapeDtypeStruct((8, D), F32),
+            jax.ShapeDtypeStruct((rows, D), F32),
+            jax.ShapeDtypeStruct((rows, D), BF),
+        ),
+        in_specs=[ANY, VM, VM, ANY, VM],
+        out_specs=(VM,) * 4,
+        scratch_shapes=[
+            pltpu.VMEM((line, shard, D), BF),
+            pltpu.VMEM((line, shard, D), BF),
+            pltpu.VMEM((2 * Z_CHIPS, a, D), BF),
+            pltpu.VMEM((Z_CHIPS, a, D), BF),
+            pltpu.VMEM((Z_CHIPS, a, D), BF),
+            pltpu.VMEM((Z_CHIPS, a, D), BF),
+            pltpu.VMEM((line, b, D), BF),
+            pltpu.VMEM((line, b, D), BF),
+            pltpu.VMEM((2, b, D), BF),
+            pltpu.VMEM((1, b, D), BF),
+            pltpu.VMEM((rows, D), BF),
+            pltpu.VMEM((4, 8, D), F32),
+            pltpu.VMEM((7, 8, D), F32),
+            dma((2, line)),
+            dma((2, line)),
+            dma((2, line)),
+            dma((2, line)),
+            dma((4, 2, line)),
+            dma((2,)),
+            dma((7,)),
+            dma((7,)),
+        ],
+        compiler_params=pltpu.CompilerParams(
+            vmem_limit_bytes=VLIM, has_side_effects=True, collective_id=1
+        ),
+    )(grads, norm_terms, place_row, gt, out_back)
 
 
 def from_partner(block, axis):
@@ -653,6 +1178,7 @@
 
 
 def per_device(
+    kernels,
     tokens,
     cotangent,
     caption_lengths,
@@ -671,57 +1197,60 @@
     total_rows = 8 * D + 2 * FF
     group_rows = total_rows // groups
     images = image_states.shape[0]
+    captions = caption_lengths.shape[1]
     axes = ("tower", "dp")
     direct = group_rows == GROUP
-    gathered = lax.all_gather(master_weights.astype(BF), axes, axis=0, tiled=True)
     ids = jnp.arange(groups, dtype=jnp.int32)
     inverse = jnp.sum(jnp.where(owner_list[None, :] == ids[:, None], ids[None, :], 0), axis=1)
+    img = image_states.reshape(-1, D)
+    if kernels:
+        gathered, x, meta, sent_cot, enc, place_row = run_gather(
+            images, caption_lengths, image_index, tokens, cotangent, img, master_weights,
+            norm_params, total_rows,
+        )
+    else:
+        gathered = lax.all_gather(master_weights.astype(BF), axes, axis=0, tiled=True)
+        place, starts, bounds = caption_plan(caption_lengths[0], image_index[0], rows, images)
+        into = (place[None, :] == jnp.arange(rows, dtype=jnp.int32)[:, None]).astype(BF)
+        meta = jnp.zeros((8, 128), jnp.int32)
+        meta = meta.at[0, :captions].set(starts)
+        meta = meta.at[0, BOUND_LANE : BOUND_LANE + images + 1].set(bounds)
+        meta = from_partner(meta, "tower")
+        x = from_partner(nn(into, tokens).astype(BF), "tower")
+        sent_cot = nn(into, cotangent).astype(BF)
+        normed, _i = normalise(img.astype(F32))
+        enc = (normed * norm_params[3] + norm_params[7]).astype(BF)
     if direct:
         slots = gathered.reshape(groups, GROUP, D)
         inv = inverse
     else:
         slots = gathered.reshape(groups, group_rows, D)[inverse].reshape(-1, GROUP, D)
         inv = jnp.arange(total_rows // GROUP, dtype=jnp.int32)
-
-    place, own_starts, own_bounds = caption_plan(caption_lengths[0], image_index[0], rows, images)
-    into = (place[None, :] == jnp.arange(rows, dtype=jnp.int32)[:, None]).astype(BF)
-    plan = from_partner(jnp.concatenate([own_starts, own_bounds]), "tower")
-    starts, bounds = plan[: own_starts.shape[0]], plan[own_starts.shape[0] :]
-    sent_tokens = jnp.dot(into, tokens, preferred_element_type=F32).astype(BF)
-    sent_cot = jnp.dot(into, cotangent, preferred_element_type=F32).astype(BF)
-    x = from_partner(sent_tokens, "tower")
     cot = from_partner(sent_cot, "tower")
-
-    img = image_states.reshape(-1, D)
-    normed, _i = normalise(img.astype(F32))
-    enc = (normed * norm_params[3] + norm_params[7]).astype(BF)
-
-    q, k, v, att, r1, cq = run_self_forward(inv, starts, x, norm_params, slots)
-    ck, cv, cross, r2 = run_cross_forward(images, inv, bounds, enc, cq, r1, slots)
+    q, k, v, att, r1, cq = run_self_forward(captions, inv, meta, x, norm_params, slots)
+    ck, cv, cross, r2 = run_cross_forward(images, inv, meta, enc, cq, r1, slots)
     out, g2, ng3, grads = run_feed_forward(inv, r2, cot, norm_params, slots)
     out_back = from_partner(out, "tower")
     g1, grad_images, ng2, grads = run_cross_backward(
-        images, inv, bounds, g2, cross, ck, cv, cq, r1, enc, img, norm_params, slots, grads
+        images, inv, meta, g2, cross, ck, cv, cq, r1, enc, img, norm_params, slots, grads
     )
     gt, ng1, grads = run_self_backward(
-        inv, starts, g1, x, q, k, v, att, norm_params, slots, grads
+        captions, inv, meta, g1, x, q, k, v, att, norm_params, slots, grads
     )
-    gt_back = from_partner(gt, "tower")
-    layer_out = lax.dot_general(
-        into, out_back, (((0,), (0,)), ((), ())), preferred_element_type=F32
-    ).astype(BF)
-    grad_tokens = lax.dot_general(
-        into, gt_back, (((0,), (0,)), ((), ())), preferred_element_type=F32
-    )
-    if direct:
-        arranged = grads.reshape(total_rows, D)
+    norm_terms = jnp.stack([ng1[0], ng2[0], ng3[0], ng2[2], ng1[1], ng2[1], ng3[1], ng2[3]])
+    if kernels:
+        reduced, norm_grads, grad_tokens, layer_out = run_sum(
+            grads.reshape(total_rows, D), norm_terms, place_row, gt, out_back
+        )
     else:
-        arranged = grads.reshape(groups, group_rows, D)[owner_list].reshape(total_rows, D)
-    reduced = lax.psum_scatter(arranged, axes, scatter_dimension=0, tiled=True).astype(F32)
-    norm_terms = jnp.stack(
-        [ng1[0], ng2[0], ng3[0], ng2[2], ng1[1], ng2[1], ng3[1], ng2[3]]
-    )
-    norm_grads = lax.psum(norm_terms, axes)
+        layer_out = tn(into, out_back).astype(BF)
+        grad_tokens = tn(into, from_partner(gt, "tower"))
+        if direct:
+            arranged = grads.reshape(total_rows, D)
+        else:
+            arranged = grads.reshape(groups, group_rows, D)[owner_list].reshape(total_rows, D)
+        reduced = lax.psum_scatter(arranged, axes, scatter_dimension=0, tiled=True).astype(F32)
+        norm_grads = lax.psum(norm_terms, axes)
     new_weights, new_first, new_second = adamw_update(
         master_weights, first_moments, second_moments, reduced, learn_rate, weight_decay
     )
@@ -747,6 +1276,12 @@
     wide = P(("tower", "dp"), None, None)
     in_specs = (split,) * 4 + (wide,) + (split,) * 3 + (P(),) * 4
     out_specs = (split, split, wide) + (split,) * 4 + (P(),) * 3
+    shape = dict(mesh.shape)
+    kernels = shape["tower"] == 2 and shape["dp"] == 4 * Z_CHIPS
     return jax.shard_map(
-        per_device, mesh=mesh, in_specs=in_specs, out_specs=out_specs, check_vma=False
+        functools.partial(per_device, kernels),
+        mesh=mesh,
+        in_specs=in_specs,
+        out_specs=out_specs,
+        check_vma=False,
     )

time: 609 us -> 452 us (0.74)
  waiting for transfers between devices: 235 us -> 0.01 us
  Pallas kernels: 229 us -> 427 us
  blocking collectives: 87 us -> 0 us
  between operations: 14.5 us -> 1.27 us
  matrix products: 10.7 us -> 0 us
  other arithmetic: 15.8 us -> 6.44 us
    pallas_call x2 -> x4, Pallas kernels: 63.6 us -> 261 us  [the longest x1 102 us: run_sum(): pl.pallas_call(sum_kernel, out_shape=(jax.ShapeDtypeStruct((shard, D), F3...]
    all_gather x1 -> x0, waiting for transfers between devices: 109 us -> none  [per_device(): lax.all_gather(master_weights.astype(BF), axes, axis=0, tiled=True)]
    reduce_scatter x1 -> x0, waiting for transfers between devices: 107 us -> none  [per_device(): lax.psum_scatter(arranged, axes, scatter_dimension=0, tiled=True)]
    psum x1 -> x0, blocking collectives: 87 us -> none  [per_device(): norm_grads = lax.psum(norm_terms, axes)]
    ppermute x5 -> x2, waiting for transfers between devices: 18.6 us -> 0.01 us  [from_partner(): lax.ppermute(block, axis, [(i, (i + half) % count) for i in range(count)])]
    dot_general x4 -> x0, matrix products: 10.7 us -> none  [the longest x1 4.06 us: per_device(): lax.dot_general(into, gt_back, (((0,), (0,)), ((), ())), preferred_elemen...]
    convert_element_type x2 -> x0, other arithmetic: 6.22 us -> none  [the longest x1 3.99 us: per_device(): enc = (normed * norm_params[3] + norm_params[7]).astype(BF)]
  transfers between devices with their start and end apart: 7 -> 2, of which waited for: 3 -> 0; matrix products, arithmetic and copies ran while one was open for 4% -> 0% of each run, Pallas kernels for 11% -> 43%
where the time goes in v2:
time: 452 us; the launch traced here: 444 us
  Pallas kernels  427 us (94%)
  local copies, waits for them, and re-layouts  7 us (2%)
  other arithmetic  6.44 us (1%)
    pallas_call x1, Pallas kernels, run_sum(): pl.pallas_call(sum_kernel, out_shape=(jax.ShapeDtypeStruct((shard, D), F3...  102 us
    pallas_call x1, Pallas kernels, run_gather(): pl.pallas_call(functools.partial(gather_kernel, images), out_shape=(jax.S...  95.9 us
    pallas_call x1, Pallas kernels, run_cross_backward(): call(functools.partial(cross_backward, images), (jax.ShapeDtypeStruct((ro...  85.1 us
    pallas_call x1, Pallas kernels, run_cross_forward(): call(functools.partial(cross_forward, images), (kv, kv, jax.ShapeDtypeStr...  43.4 us
    pallas_call x1, Pallas kernels, run_self_backward(): call(functools.partial(self_backward, captions), (jax.ShapeDtypeStruct((r...  37.4 us
    pallas_call x1, Pallas kernels, run_feed_forward(): call(feed_forward, (jax.ShapeDtypeStruct((rows, D), BF), jax.ShapeDtypeSt...  37 us
    pallas_call x1, Pallas kernels, run_self_forward(): call(functools.partial(self_forward, captions), (one, one, one, one, jax....  26.2 us
  transfers between devices with their start and end apart: 2, of which 0 were waited for; matrix products, arithmetic and copies ran while one was open for 0% of the time, Pallas kernels for 43%

profile of v2, /device:TPU:0, one launch (start us, length us, event | category | flops | bytes accessed | tf_op | source)
XLA Modules:
  0.0 443.6 jit_solution(1691828186903998427)
XLA Ops:
  0.6 0.0 copy-start.12
  0.7 95.9 %shard_map.195 = (bf16[12288,768]{1,0:T(8,128)(2,1)}, bf16[768,768]{1,0:T(8,128)(2,1)}, s32[8,128]{1,0:T(8,128)}, bf16[768,768]{1,0:T(8,128)(2,1)}, bf16[2304,768]{1,0:T(8,128)(2,1)}, /*index=5*/s32[8,768]{1,0:T(8,128)}) custom-call(s32[1,24]{1,0:T(1,128)} %lengths.1, s32[1,24]{1,0:T(1,128)} %picks.1, bf16[768,768]{1,0:T(8,128)(2,1)} %tokens.1, ...), custom_call_target="tpu_custom_call" | custom-call | tf_op jit(solution)/shard_map/pallas_call | solution.py:900
  96.5 1.6 collective-permute-start
  98.1 0.0 copy-done.12
  98.1 0.6 select_reduce_fusion.inv
  98.7 26.2 %shard_map.196 = (bf16[768,768]{1,0:T(8,128)(2,1)}, bf16[768,768]{1,0:T(8,128)(2,1)}, bf16[768,768]{1,0:T(8,128)(2,1)}, bf16[768,768]{1,0:T(8,128)(2,1)}, f32[768,768]{1,0:T(8,128)}, /*index=5*/bf16[768,768]{1,0:T(8,128)(2,1)}) custom-call(s32[64]{0:T(128)} %select_reduce_fusion.inv, s32[8,128]{1,0:T(8,128)} %get-tuple-element.41.meta, ...), custom_call_target="tpu_custom_call" | custom-call | tf_op jit(solution)/shard_map/pallas_call | solution.py:199
  125.0 43.4 %shard_map.197 = (bf16[2304,768]{1,0:T(8,128)(2,1)}, bf16[2304,768]{1,0:T(8,128)(2,1)}, bf16[768,768]{1,0:T(8,128)(2,1)}, f32[768,768]{1,0:T(8,128)}) custom-call(s32[64]{0:T(128)} %select_reduce_fusion.inv, s32[8,128]{1,0:T(8,128)} %get-tuple-element.41.meta, bf16[2304,768]{1,0:T(8,128)(2,1)} %get-tuple-element.42.enc, ...), custom_call_target="tpu_custom_call" | custom-call | tf_op jit(solution)/shard_map/pallas_call | solution.py:272
  168.4 0.0 collective-permute-done.cot
  168.4 0.0 copy-start.6
  168.4 1.0 copy-done.6
  169.4 37.0 %shard_map.198 = (bf16[768,768]{1,0:T(8,128)(2,1)}, f32[768,768]{1,0:T(8,128)}, f32[2,768]{1,0:T(2,128)}, bf16[64,192,768]{2,1,0:T(8,128)(2,1)}) custom-call(s32[64]{0:T(128)} %select_reduce_fusion.inv, f32[768,768]{1,0:T(8,128)} %get-tuple-element.47.r2, bf16[768,768]{1,0:T(8,128)(2,1)} %copy-done.6, f32[8,768]{1,0:T(8,128)} %norms.9, ...), custom_call_target="tpu_custom_call" | custom-call | tf_op jit(solution)/shard_map/pallas_call | solution.py:377
  206.4 0.6 collective-permute-start.1
  207.0 85.1 %shard_map.199 = (f32[768,768]{1,0:T(8,128)}, f32[2304,768]{1,0:T(8,128)}, f32[4,768]{1,0:T(4,128)}, bf16[64,192,768]{2,1,0:T(8,128)(2,1)}) custom-call(s32[64]{0:T(128)} %select_reduce_fusion.inv, s32[8,128]{1,0:T(8,128)} %get-tuple-element.41.meta, f32[768,768]{1,0:T(8,128)} %get-tuple-element.49.g2, ...), custom_call_target="tpu_custom_call", output_to_operand_aliasing={{3}: (12, {})} | custom-call | tf_op jit(solution)/shard_map/pallas_call | solution.py:506
  292.1 0.0 copy-start.11
  292.1 0.0 copy-start.10
  292.1 37.4 %shard_map.200 = (bf16[768,768]{1,0:T(8,128)(2,1)}, f32[2,768]{1,0:T(2,128)}, bf16[64,192,768]{2,1,0:T(8,128)(2,1)}) custom-call(s32[64]{0:T(128)} %select_reduce_fusion.inv, s32[8,128]{1,0:T(8,128)} %get-tuple-element.41.meta, f32[768,768]{1,0:T(8,128)} %get-tuple-element.54.g1, ...), custom_call_target="tpu_custom_call", output_to_operand_aliasing={{2}: (10, {})} | custom-call | tf_op jit(solution)/shard_map/pallas_call | solution.py:608
  329.4 0.0 copy-done.11
  329.5 0.0 copy-done.10
  329.5 0.8 fusion.5
  330.3 0.7 stack.3.norm_terms
  330.9 0.0 collective-permute-done.1.out_back
  330.9 0.0 copy-start.4
  330.9 1.0 copy-done.4
  331.9 0.0 copy-start.7
  331.9 0.0 copy-start.8
  331.9 0.0 copy-start.9
  331.9 0.0 copy-start
  331.9 0.0 copy-start.2
  332.0 0.0 copy-start.3
  332.0 101.8 %shard_map.201 = (f32[384,768]{1,0:T(8,128)}, f32[8,768]{1,0:T(8,128)}, f32[768,768]{1,0:T(8,128)}, bf16[768,768]{1,0:T(8,128)(2,1)}) custom-call(bf16[12288,768]{1,0:T(8,128)(2,1)} %bitcast.9, f32[8,768]{1,0:T(8,128)} %stack.3.norm_terms, s32[8,768]{1,0:T(8,128)} %get-tuple-element.64.place_row, bf16[768,768]{1,0:T(8,128)(2,1)} %get-tuple-element.65.gt, ...), custom_call_target="tpu_custom_call" | custom-call | tf_op jit(solution)/shard_map/pallas_call | solution.py:1110
  433.8 0.0 copy-done.7
  433.8 0.0 copy-done.8
  433.8 0.0 copy-done.9
  433.8 1.4 multiply_subtract_fusion.1
  435.2 0.0 copy-done
  435.2 0.0 copy-done.2
  435.2 0.0 copy-done.3
  435.2 0.0 copy-start.5
  435.2 4.4 fusion.3
  439.6 0.0 copy-done.5
  439.6 0.0 copy-start.1
  439.6 1.0 copy.28
  440.6 1.1 copy-done.1
  441.7 1.4 copy.29
  (1 shorter events, 0.0 us)
Async XLA Ops:
  0.6 97.4 %copy-start.12 = (s32[64]{0:T(128)S(1)}, s32[64]{0:T(128)}, u32[]{:S(2)}) copy-start(s32[64]{0:T(128)} %param.20) | copy-start | bytes 772
  96.5 71.9 %collective-permute-start = (bf16[768,768]{1,0:T(8,128)(2,1)}, bf16[768,768]{1,0:T(8,128)(2,1)S(1)}, u32[]{:S(2)}, u32[]{:S(2)}) collective-permute-start(bf16[768,768]{1,0:T(8,128)(2,1)} %get-tuple-element.48), channel_id=1, source_target_pairs={{0,16},{16,0},{1,17},{17,1},{2,18},{18,2},{3,19},{19,3},{4,20},{20... | collective-permute-start | bytes 3538952 | tf_op jit(solution)/shard_map/ppermute | solution.py:1152
  168.4 1.0 copy-start.6
  206.4 124.5 %collective-permute-start.1 = (bf16[768,768]{1,0:T(8,128)(2,1)}, bf16[768,768]{1,0:T(8,128)(2,1)S(1)}, u32[]{:S(2)}, u32[]{:S(2)}) collective-permute-start(bf16[768,768]{1,0:T(8,128)(2,1)} %get-tuple-element.66), channel_id=1, source_target_pairs={{0,16},{16,0},{1,17},{17,1},{2,18},{18,2},{3,19},{19,3},{4,20},{20... | collective-permute-start | bytes 3538952 | tf_op jit(solution)/shard_map/ppermute | solution.py:1152
  292.1 37.4 %copy-start.11 = (f32[2,768]{1,0:T(2,128)S(1)}, f32[2,768]{1,0:T(2,128)}, u32[]{:S(2)}) copy-start(f32[2,768]{1,0:T(2,128)} %get-tuple-element.63) | copy-start | bytes 18436
  292.1 37.4 %copy-start.10 = (f32[4,768]{1,0:T(4,128)S(1)}, f32[4,768]{1,0:T(4,128)}, u32[]{:S(2)}) copy-start(f32[4,768]{1,0:T(4,128)} %get-tuple-element.62) | copy-start | bytes 36868
  330.9 1.0 copy-start.4
  331.9 101.8 %copy-start.7 = (f32[8,768]{1,0:T(8,128)S(1)}, f32[8,768]{1,0:T(8,128)}, u32[]{:S(2)}) copy-start(f32[8,768]{1,0:T(8,128)} %norms.9) | copy-start | bytes 73732
  331.9 101.8 %copy-start.8 = (f32[8,768]{1,0:T(8,128)S(1)}, f32[8,768]{1,0:T(8,128)}, u32[]{:S(2)}) copy-start(f32[8,768]{1,0:T(8,128)} %param.22) | copy-start | bytes 73732
  331.9 101.8 %copy-start.9 = (f32[8,768]{1,0:T(8,128)S(1)}, f32[8,768]{1,0:T(8,128)}, u32[]{:S(2)}) copy-start(f32[8,768]{1,0:T(8,128)} %param.23) | copy-start | bytes 73732
  331.9 103.2 %copy-start = (f32[384,768]{1,0:T(8,128)S(1)}, f32[384,768]{1,0:T(8,128)}, u32[]{:S(2)}) copy-start(f32[384,768]{1,0:T(8,128)} %master.1) | copy-start | bytes 3538948
  331.9 103.2 %copy-start.2 = (f32[384,768]{1,0:T(8,128)S(1)}, f32[384,768]{1,0:T(8,128)}, u32[]{:S(2)}) copy-start(f32[384,768]{1,0:T(8,128)} %param.18) | copy-start | bytes 3538948
  332.0 103.2 %copy-start.3 = (f32[384,768]{1,0:T(8,128)S(1)}, f32[384,768]{1,0:T(8,128)}, u32[]{:S(2)}) copy-start(f32[384,768]{1,0:T(8,128)} %param.19) | copy-start | bytes 3538948
  435.2 4.4 %copy-start.5 = (bf16[768,768]{1,0:T(8,128)(2,1)S(1)}, bf16[768,768]{1,0:T(8,128)(2,1)}, u32[]{:S(2)}) copy-start(bf16[768,768]{1,0:T(8,128)(2,1)} %get-tuple-element.99) | copy-start | bytes 3538948
  439.6 2.1 copy-start.1
